TPU v7x, 256 devices: a whole 4x4x8 slice. The times are simulated.
256 devices in a mesh: beam: 16 (over x, y), tensor: 16 (over z, core).
Axes of the slice: x: 4, y: 4, z: 8, core: 2. Of those that a mesh axis runs over, the one named last changes fastest.
Arguments:
- ssm_state: float32 [16, 8, 16, 16384], P('beam', None, None, 'tensor'), may hold values from -6 to 6
- conv_state: bfloat16 [16, 8, 3, 16384], P('beam', None, None, 'tensor'), may hold values from -6 to 6
- suffix_kv: bfloat16 [16, 8, 16, 4096], P('beam', None, None, 'tensor'), may hold values from -4 to 4
- mamba_x: bfloat16 [2, 16, 8, 16384], P(None, 'beam', None, 'tensor'), may hold values from -6 to 6
- mamba_gate: bfloat16 [2, 16, 8, 16384], P(None, 'beam', None, 'tensor'), may hold values from -6 to 6
- conv_weight: bfloat16 [4, 16384], P(None, 'tensor'), may hold values from -3 to 3
- conv_bias: bfloat16 [16384], P('tensor'), may hold values from -3 to 3
- xproj_weight: bfloat16 [16384, 288], P('tensor'), may hold values from -0.046875 to 0.046875
- dt_gain: float32 [256], replicated, may hold values from 0.25 to 1.75
- dtproj_weight: bfloat16 [256, 16384], P(None, 'tensor'), may hold values from -0.375 to 0.375
- dt_bias: float32 [16384], P('tensor'), may hold values from -3 to 1
- state_rates: float32 [16, 16384], P(None, 'tensor'), may hold values from 0.05 to 4
- skip_gain: float32 [16384], P('tensor'), may hold values from 0.5 to 1.5
- queries: bfloat16 [2, 16, 8, 8192], P(None, 'beam', None, 'tensor'), may hold values from -32 to 32
- new_kv: bfloat16 [2, 16, 8, 4096], P(None, 'beam', None, 'tensor'), may hold values from -4 to 4
- kv_pool: bfloat16 [4096, 16, 4096], P('beam', None, 'tensor'), may hold values from -4 to 4
- page_order: int32 [4096], replicated, may hold values from 0 to 4095, each once
- ctx_len: int32 [8], replicated, may hold values from 1 to 8192, 32768 in all
- parents: int32 [2, 16, 8, 1], replicated, may hold values from 0 to 15; in each aligned block of 8 rows (0 to 7, 8 to 15, ..., all dimensions but the last counted through in order) at most 2 rows name the same one
Outputs:
- mamba_out: bfloat16 [2, 16, 8, 16384], P(None, 'beam', None, 'tensor')
- attn_out: bfloat16 [2, 16, 8, 8192], P(None, 'beam', None, 'tensor')
Inputs may be any that keep to these rules, and one draw needn't show every extreme that they name: parents[s, b, r, 0] is the beam whose state and own tokens beam b of request r continues at step s; for one step and one child beam b, no beam is the parent of more than 2 of the 8 requests, and some beam is the parent of exactly 2. `ctx_len`: the longest prefix has exactly 8192 tokens, and all sum to 32768. `page_order`: each pool page appears once.
All inputs are finite; a program needn't handle non-finite values.
Results may differ from a plain program's by a relative error of at most 0.019.
Values may be sent and summed in bfloat16 or wider, within the bound.
A program may use at most 128 MiB of HBM per device.

v0:
```python
import jax
import jax.numpy as jnp
from jax import lax
from jax.sharding import PartitionSpec as P

DS = 16
DT_RANK = 256
HD = 128
STEPS = 2
PAGE = 16
MAXP = 512


def slot_plan(parent_now, own_beam, capacity):
    requests = parent_now.shape[1]
    chosen = parent_now == own_beam
    ranking = jnp.cumsum(chosen.astype(jnp.int32), axis=1) - 1
    slot_ids = jnp.arange(capacity, dtype=jnp.int32)
    picked = chosen[:, None, :] & (ranking[:, None, :] == slot_ids[None, :, None])
    row_ids = jnp.arange(requests, dtype=jnp.int32)
    source_row = jnp.sum(picked.astype(jnp.int32) * row_ids[None, None, :], axis=2).reshape(-1)
    filled = jnp.any(picked, axis=2).reshape(-1)
    own_parents = lax.dynamic_index_in_dim(parent_now, own_beam, 0, keepdims=False)
    alike = own_parents[:, None] == own_parents[None, :]
    before = row_ids[None, :] < row_ids[:, None]
    ordering = jnp.sum((alike & before).astype(jnp.int32), axis=1)
    return (source_row, filled, own_parents, ordering)


def pack_slots(source, source_row, filled):
    gathered = jnp.take(source, source_row, axis=0)
    keep_mask = filled.reshape((-1,) + (1,) * (gathered.ndim - 1))
    return jnp.where(keep_mask, gathered, jnp.zeros_like(gathered))


def local(
    ssm_state,
    conv_state,
    suffix_kv,
    mamba_x,
    mamba_gate,
    conv_weight,
    conv_bias,
    xproj_weight,
    dt_gain,
    dtproj_weight,
    dt_bias,
    state_rates,
    skip_gain,
    queries,
    new_kv,
    kv_pool,
    page_order,
    ctx_len,
    parents,
):
    own_beam = lax.axis_index("beam")
    beams = lax.axis_size("beam")
    requests = ssm_state.shape[1]
    capacity = max(2, 3 * requests // (2 * beams))
    local_pages = kv_pool.shape[0]
    slots = kv_pool.shape[-1] // (2 * HD)
    group = queries.shape[-1] // HD // slots
    score_scale = HD ** (-0.5)
    inverse = jnp.argsort(page_order)
    local_ids = lax.dynamic_slice_in_dim(inverse, own_beam * local_pages, local_pages)
    page_request = local_ids // MAXP
    positions = (local_ids % MAXP)[:, None] * PAGE + jnp.arange(PAGE, dtype=jnp.int32)[None, :]
    visible = positions < jnp.take(ctx_len, page_request)[:, None]
    visible_mask = visible[None, :, None, None, :]
    request_ids = jnp.arange(requests, dtype=jnp.int32)
    member = request_ids[:, None] == page_request[None, :]
    member_float = member.astype(jnp.float32)
    own_row = (jnp.arange(beams, dtype=jnp.int32) == own_beam)[:, None, None, None]
    page_rows = kv_pool.reshape(local_pages, PAGE, slots, 2, HD)
    all_queries = lax.all_gather(queries, "beam", axis=1, tiled=True)
    ssm_now = ssm_state[0]
    window = conv_state[0]
    suffix = suffix_kv[0]
    conv_kernel = conv_weight.astype(jnp.float32)
    conv_shift = conv_bias.astype(jnp.float32)
    mamba_steps = []
    attn_steps = []
    for decode_step in range(STEPS):
        parent_now = parents[decode_step, :, :, 0]
        source_row, filled, own_parents, ordering = slot_plan(parent_now, own_beam, capacity)
        got_state = lax.all_to_all(
            pack_slots(ssm_now, source_row, filled), "beam", split_axis=0, concat_axis=0, tiled=True
        )
        got_window, got_suffix = (
            lax.all_to_all(
                pack_slots(window, source_row, filled),
                "beam",
                split_axis=0,
                concat_axis=0,
                tiled=True,
            ),
            lax.all_to_all(
                pack_slots(suffix, source_row, filled),
                "beam",
                split_axis=0,
                concat_axis=0,
                tiled=True,
            ),
        )
        landing = own_parents * capacity + ordering
        carried = jnp.take(got_state, landing, axis=0)
        window_old = jnp.take(got_window, landing, axis=0)
        suffix_old = jnp.take(got_suffix, landing, axis=0)
        window_full = jnp.concatenate([window_old, mamba_x[decode_step, 0][:, None, :]], axis=1)
        window = window_full[:, 1:]
        conv_out = jax.nn.silu(
            jnp.sum(window_full.astype(jnp.float32) * conv_kernel[None], axis=1) + conv_shift
        )
        partial_value = jnp.dot(
            conv_out.astype(jnp.bfloat16), xproj_weight, preferred_element_type=jnp.float32
        )
        projected = lax.psum(partial_value, "tensor")
        rank_part = projected[:, :DT_RANK]
        input_map = projected[:, DT_RANK : DT_RANK + DS]
        output_map = projected[:, DT_RANK + DS :]
        rank_norm = (
            rank_part
            * lax.rsqrt(jnp.mean(rank_part * rank_part, axis=-1, keepdims=True) + 1e-06)
            * dt_gain
        ).astype(jnp.bfloat16)
        step_size = jax.nn.softplus(
            jnp.dot(rank_norm, dtproj_weight, preferred_element_type=jnp.float32) + dt_bias
        )
        ssm_now = (
            jnp.exp(-step_size[:, None, :] * state_rates[None]) * carried
            + (step_size * conv_out)[:, None, :] * input_map[:, :, None]
        )
        mixture = jnp.sum(output_map[:, :, None] * ssm_now, axis=1) + skip_gain * conv_out
        mamba_steps.append(
            (mixture * jax.nn.silu(mamba_gate[decode_step, 0].astype(jnp.float32))).astype(
                jnp.bfloat16
            )
        )
        suffix = jnp.concatenate([suffix_old, new_kv[decode_step, 0][:, None, :]], axis=1)
        page_queries = jnp.take(all_queries[decode_step], page_request, axis=1).reshape(
            beams, local_pages, slots, group, HD
        )
        prefix_scores = (
            jnp.einsum(
                "bpcgd,ptcd->bpcgt",
                page_queries,
                page_rows[:, :, :, 0],
                preferred_element_type=jnp.float32,
            )
            * score_scale
        )
        prefix_scores = jnp.where(visible_mask, prefix_scores, -jnp.inf)
        suffix_rows = suffix.reshape(requests, -1, slots, 2, HD)
        own_heads = queries[decode_step, 0].reshape(requests, slots, group, HD)
        suffix_scores = (
            jnp.einsum(
                "rcgd,rtcd->rcgt",
                own_heads,
                suffix_rows[:, :, :, 0],
                preferred_element_type=jnp.float32,
            )
            * score_scale
        )
        page_top = jnp.max(prefix_scores, axis=-1)
        request_top = jnp.max(
            jnp.where(member[None, :, :, None, None], page_top[:, None], -jnp.inf), axis=2
        )
        suffix_top = jnp.max(suffix_scores, axis=-1)
        local_top = jnp.where(own_row, jnp.maximum(request_top, suffix_top[None]), request_top)
        highest = lax.pmax(local_top, "beam")
        page_high = jnp.take(highest, page_request, axis=1)
        prefix_exp = jnp.where(visible_mask, jnp.exp(prefix_scores - page_high[..., None]), 0.0)
        own_high = lax.dynamic_index_in_dim(highest, own_beam, 0, keepdims=False)
        suffix_exp = jnp.exp(suffix_scores - own_high[..., None])
        request_sum = jnp.einsum(
            "rp,bpcg->brcg",
            member_float,
            jnp.sum(prefix_exp, axis=-1),
            precision=lax.Precision.HIGHEST,
        )
        local_sum = request_sum + jnp.where(own_row, jnp.sum(suffix_exp, axis=-1)[None], 0.0)
        normaliser = lax.psum(local_sum, "beam")
        page_norm = jnp.take(normaliser, page_request, axis=1)
        prefix_weights = (prefix_exp / page_norm[..., None]).astype(jnp.bfloat16)
        page_values = jnp.einsum(
            "bpcgt,ptcd->bpcgd",
            prefix_weights,
            page_rows[:, :, :, 1],
            preferred_element_type=jnp.float32,
        )
        request_values = jnp.einsum(
            "rp,bpcgd->brcgd", member_float, page_values, precision=lax.Precision.HIGHEST
        )
        prefix_total = lax.psum_scatter(
            request_values.reshape(beams, requests, -1).astype(jnp.bfloat16),
            "beam",
            scatter_dimension=0,
            tiled=True,
        ).astype(jnp.float32)
        own_norm = lax.dynamic_index_in_dim(normaliser, own_beam, 0, keepdims=False)
        suffix_weights = (suffix_exp / own_norm[..., None]).astype(jnp.bfloat16)
        suffix_values = jnp.einsum(
            "rcgt,rtcd->rcgd",
            suffix_weights,
            suffix_rows[:, :, :, 1],
            preferred_element_type=jnp.float32,
        )
        attn_steps.append(
            (prefix_total[0] + suffix_values.reshape(requests, -1)).astype(jnp.bfloat16)
        )
    return (jnp.stack(mamba_steps)[:, None], jnp.stack(attn_steps)[:, None])


def solution(mesh):
    in_specs = (
        P("beam", None, None, "tensor"),
        P("beam", None, None, "tensor"),
        P("beam", None, None, "tensor"),
        P(None, "beam", None, "tensor"),
        P(None, "beam", None, "tensor"),
        P(None, "tensor"),
        P("tensor"),
        P("tensor", None),
        P(),
        P(None, "tensor"),
        P("tensor"),
        P(None, "tensor"),
        P("tensor"),
        P(None, "beam", None, "tensor"),
        P(None, "beam", None, "tensor"),
        P("beam", None, "tensor"),
        P(),
        P(),
        P(),
    )
    out_specs = (P(None, "beam", None, "tensor"), P(None, "beam", None, "tensor"))
    return jax.shard_map(local, mesh=mesh, in_specs=in_specs, out_specs=out_specs, check_vma=False)
```

profile of v0, /device:TPU:2, one launch (start us, length us, event | category | flops | bytes accessed | tf_op | source)
XLA Modules:
  0.0 601.7 jit_solution(8747366216472243894)
XLA Ops:
  11.1 7.5 %all-to-all-start = ((bf16[32,3,1024]{2,1,0:T(4,128)(2,1)}), bf16[32,3,1024]{2,1,0:T(4,128)(2,1)}, u32[]{:S(2)}, u32[]{:S(2)}) async-start(bf16[32,3,1024]{2,1,0:T(4,128)(2,1)} %select_select_fusion.4), calls=%async_computation | async-start | bytes 524288 | tf_op jit(solution)/shard_map/all_to_all | solution.py:91
  21.9 6.5 %sort.17 = (s32[4096]{0:T(1024)}, s32[4096]{0:T(1024)S(1)}) sort(s32[4096]{0:T(1024)} %param.47, s32[4096]{0:T(1024)S(1)} %iota.40), dimensions={0}, to_apply=%region_16.21 | sort | flops 49152 | bytes 65536 | tf_op jit(solution)/shard_map/jit(argsort)/sort | solution.py:65
  28.4 5.8 fusion.123
  50.9 23.4 %all_gather.3 = bf16[2,16,8,512]{3,2,0,1:T(8,128)(2,1)S(1)} all-gather(bf16[2,1,8,512]{3,2,0,1:T(8,128)(2,1)} %bitcast.342), channel_id=1, replica_groups=mesh['beam'=16,'tensor'=16] {'beam'}, dimensions={1}, use_global_device_ids=true | all-gather | bytes 278528 | tf_op jit(solution)/shard_map/all_gather | solution.py:76
  77.5 3.5 copy.164
  93.6 5.5 select_bitcast_fusion
  99.0 9.9 %fusion.10 = f32[256,16,4,16]{1,3,2,0:T(8,128)S(1)} fusion(bf16[256,2,4,8,128]{4,3,2,1,0:T(8,128)(2,1)S(1)} %get-tuple-element.82, bf16[256,16,1,1,128]{4,1,0,3,2:T(8,128)(2,1)S(1)} %copy-done.3), kind=kOutput, calls=%fused_computation.34 | convolution fusion | flops 67108864 | bytes 6291456 | tf_op jit(solution)/shard_map/bpcgd,ptcd->bpcgt/dot_general | solution.py:145
  109.0 16.9 %fusion.6 = (f32[16,256,4]{0,2,1:T(4,128)}, f32[16,256,4]{0,2,1:T(4,128)S(1)}, f32[256,16,4,16]{1,3,2,0:T(8,128)}) fusion(pred[256,16]{1,0:T(8,128)(4,1)S(1)} %add_compare_fusion, f32[256,16,4,16]{1,3,2,0:T(8,128)S(1)} %fusion.10, bf16[256,16,1,1,128]{4,1,0,3,2:T(8,128)(2,1)} %copy.212, bf16[256,2,4,8,128]{4,3,2,1,0:T(8,128)(2,1)} %get-tuple-element.83), kind=kOutput, calls=%fused_computation.30 | convolution fusion | flops 68648960 | bytes 7475200 | tf_op jit(solution)/shard_map/bpcgd,ptcd->bpcgt/dot_general | solution.py:145
  129.1 5.7 all-to-all-start.4
  138.5 3.0 all-to-all-done.4
  141.6 5.3 all-to-all-start.2
  153.8 5.2 all-to-all-start.5
  160.8 48.6 %all-reduce.2 = (f32[8,288]{1,0:T(8,128)S(1)}, f32[8,288]{1,0:T(8,128)S(1)}) all-reduce(f32[8,288]{1,0:T(8,128)S(1)} %fusion.95, f32[8,288]{1,0:T(8,128)S(1)} %fusion.93), channel_id=1, replica_groups=mesh['beam'=16,'tensor'=16] {'tensor'}, use_global_device_ids=true, to_apply=%region_5.8 | all-reduce | flops 4608 | bytes 36864 | tf_op jit(solution)/shard_map/psum | solution.py:118
  211.6 7.2 %all-to-all-start.1 = ((f32[32,16,1024]{2,1,0:T(8,128)}), f32[32,16,1024]{2,1,0:T(8,128)S(1)}, u32[]{:S(2)}, u32[]{:S(2)}) async-start(f32[32,16,1024]{2,1,0:T(8,128)} %select_select_fusion.1), calls=%async_computation.1 | async-start | bytes 4194304 | tf_op jit(solution)/shard_map/all_to_all | solution.py:87
  223.1 79.1 %all-reduce.4 = (f32[16,8,1,4]{0,1,3,2:T(8,128)S(1)}, f32[16,8,1,4]{0,1,3,2:T(8,128)S(1)}) all-reduce(f32[16,8,1,4]{0,1,3,2:T(8,128)S(1)} %get-tuple-element.81, f32[16,8,1,4]{0,1,3,2:T(8,128)S(1)} %get-tuple-element.80), channel_id=1, replica_groups=mesh['beam'=16,'tensor'=16] {'beam'}, use_global_device_ids=true, to_apply=%region_20.26 | all-reduce | flops 1024 | bytes 8192 | tf_op jit(solution)/shard_map/pmax | solution.py:171
  306.3 10.7 %fusion.8 = (f32[16,256,4]{0,2,1:T(4,128)S(1)}, f32[16,256,4]{0,2,1:T(4,128)S(1)}) fusion(f32[256,16,4,16]{1,3,2,0:T(8,128)} %get-tuple-element.92, f32[16,256,4]{0,2,1:T(4,128)S(1)} %get-tuple-element.79, pred[256,16]{1,0:T(8,128)(4,1)S(1)} %add_compare_fusion, f32[16,256,4]{0,2,1:T(4,128)S(1)} %get-tuple-element.78, f32[256,16,4,16]{1,3,2,0:T(8,128)} %copy-done.2), kind=kLoop, calls=%fused_computation.32 | loop fusion | flops 2588672 | bytes 2363392 | tf_op jit(solution)/shard_map/reduce_sum | solution.py:179
  317.6 69.8 %all-reduce.3 = (f32[16,8,1,4]{0,1,3,2:T(8,128)S(1)}, f32[16,8,1,4]{0,1,3,2:T(8,128)S(1)}) all-reduce(f32[16,8,1,4]{0,1,3,2:T(8,128)S(1)} %fusion.51, f32[16,8,1,4]{0,1,3,2:T(8,128)S(1)} %fusion.50), channel_id=1, replica_groups=mesh['beam'=16,'tensor'=16] {'beam'}, use_global_device_ids=true, to_apply=%region_31.38 | all-reduce | flops 1024 | bytes 8192 | tf_op jit(solution)/shard_map/psum | solution.py:183
  390.5 8.1 %fusion.35 = f32[16,256,4,128]{3,0,2,1:T(8,128)} fusion(f32[16,256,4]{0,2,1:T(4,128)S(1)} %get-tuple-element.77, f32[256,16,4,16]{1,3,2,0:T(8,128)} %copy-done.2, f32[16,256,4]{0,2,1:T(4,128)} %copy-done.7, pred[256,16]{1,0:T(8,128)(4,1)S(1)} %add_compare_fusion, bf16[256,16,1,1,128]{4,1,0,3,2:T(8,128)(2,1)} %copy.213), kind=kOutput, calls=%fused_computation.59 | convolution fusion | flops 68681728 | bytes 10620928 | tf_op jit(solution)/shard_map/bpcgt,ptcd->bpcgd/dot_general | solution.py:186
  399.5 8.0 %fusion.32 = f32[16,256,4,128]{3,0,2,1:T(8,128)} fusion(f32[16,256,4]{0,2,1:T(4,128)S(1)} %copy-done.10, f32[256,16,4,16]{1,3,2,0:T(8,128)} %get-tuple-element.92, f32[16,256,4]{0,2,1:T(4,128)S(1)} %copy-done.6, pred[256,16]{1,0:T(8,128)(4,1)S(1)} %add_compare_fusion, bf16[256,16,1,1,128]{4,1,0,3,2:T(8,128)(2,1)} %copy.213), kind=kOutput, calls=%fused_computation.58 | convolution fusion | flops 68681728 | bytes 10620928 | tf_op jit(solution)/shard_map/bpcgt,ptcd->bpcgd/dot_general | solution.py:186
  410.9 10.1 %all-to-all-start.3 = ((f32[32,16,1024]{2,1,0:T(8,128)}), f32[32,16,1024]{2,1,0:T(8,128)S(1)}, u32[]{:S(2)}, u32[]{:S(2)}) async-start(f32[32,16,1024]{2,1,0:T(8,128)} %select_select_fusion), calls=%async_computation.3 | async-start | bytes 4194304 | tf_op jit(solution)/shard_map/all_to_all | solution.py:87
  421.5 11.8 %fusion.47 = bf16[16,8,512]{2,1,0:T(8,128)(2,1)} fusion(f32[16,256,4,128]{3,0,2,1:T(8,128)} %fusion.32, s32[256]{0:T(256)S(1)} %get-tuple-element.39), kind=kOutput, calls=%fused_computation.65 | convolution fusion | flops 201394176 | bytes 8520704 | tf_op jit(solution)/shard_map/rp,bpcgd->brcgd/dot_general | solution.py:192
  433.9 11.8 %fusion.44 = bf16[16,8,512]{2,1,0:T(8,128)(2,1)} fusion(f32[16,256,4,128]{3,0,2,1:T(8,128)} %fusion.35, s32[256]{0:T(256)S(1)} %get-tuple-element.39), kind=kOutput, calls=%fused_computation.64 | convolution fusion | flops 201394176 | bytes 8520704 | tf_op jit(solution)/shard_map/rp,bpcgd->brcgd/dot_general | solution.py:192
  446.3 63.8 %reduce-scatter.7.cloned.1.call-done = bf16[1,8,512]{2,1,0:T(8,128)(2,1)} async-done(((bf16[16,8,512]{2,1,0:T(8,128)(2,1)}), bf16[1,8,512]{2,1,0:T(8,128)(2,1)}) %reduce-scatter.7.cloned.1.call-update) | async-done | bytes 8208
  510.7 79.3 %reduce-scatter.9.cloned.1.call-done = bf16[1,8,512]{2,1,0:T(8,128)(2,1)} async-done(((bf16[16,8,512]{2,1,0:T(8,128)(2,1)}), bf16[1,8,512]{2,1,0:T(8,128)(2,1)}) %reduce-scatter.9.cloned.1.call-update) | async-done | bytes 8208
  (265 shorter events, 79.7 us)
Async XLA Ops:
  7.2 153.1 %copy-start = (bf16[1024,288]{0,1:T(8,128)(2,1)S(1)}, bf16[1024,288]{0,1:T(8,128)(2,1)}, u32[]{:S(2)}) copy-start(bf16[1024,288]{0,1:T(8,128)(2,1)} %param.38) | copy-start | bytes 1769476
  7.2 67.1 %copy-start.4 = (f32[1,8,16,1024]{3,2,1,0:T(8,128)S(1)}, f32[1,8,16,1024]{3,2,1,0:T(8,128)}, u32[]{:S(2)}) copy-start(f32[1,8,16,1024]{3,2,1,0:T(8,128)} %param.31) | copy-start | bytes 1572868
  8.3 42.6 %copy-start.46 = (pred[32]{0:T(512)(128)(4,1)}, pred[32]{0:T(512)(128)(4,1)S(1)}, u32[]{:S(2)}) copy-start(pred[32]{0:T(512)(128)(4,1)S(1)} %compare_and_fusion.3) | copy-start | bytes 100
  8.5 42.4 %copy-start.39 = (pred[32]{0:T(512)(128)(4,1)}, pred[32]{0:T(512)(128)(4,1)S(1)}, u32[]{:S(2)}) copy-start(pred[32]{0:T(512)(128)(4,1)S(1)} %broadcast_in_dim.320) | copy-start | bytes 100
  8.5 38.7 %copy-start.40 = (s32[1024]{0:T(1024)}, s32[1024]{0:T(1024)S(1)}, u32[]{:S(2)}) copy-start(s32[1024]{0:T(1024)S(1)} %pad_clamp_fusion.8) | copy-start | bytes 12292
  11.1 117.9 %all-to-all-start = ((bf16[32,3,1024]{2,1,0:T(4,128)(2,1)}), bf16[32,3,1024]{2,1,0:T(4,128)(2,1)}, u32[]{:S(2)}, u32[]{:S(2)}) async-start(bf16[32,3,1024]{2,1,0:T(4,128)(2,1)} %select_select_fusion.4), calls=%async_computation | async-start | bytes 524288 | tf_op jit(solution)/shard_map/all_to_all | solution.py:91
  127.1 83.1 %copy-start.8 = (bf16[256,1024]{1,0:T(8,128)(2,1)S(1)}, bf16[256,1024]{1,0:T(8,128)(2,1)}, u32[]{:S(2)}) copy-start(bf16[256,1024]{1,0:T(8,128)(2,1)} %param.40) | copy-start | bytes 1572868
  127.2 83.1 %copy-start.20 = (f32[1024]{0:T(1024)S(1)}, f32[1024]{0:T(1024)}, u32[]{:S(2)}) copy-start(f32[1024]{0:T(1024)} %param.41) | copy-start | bytes 12292
  127.2 83.1 %copy-start.47 = (f32[256]{0:T(256)S(1)}, f32[256]{0:T(256)}, u32[]{:S(2)}) copy-start(f32[256]{0:T(256)} %param.39) | copy-start | bytes 3076
  129.0 81.8 %copy-start.44 = (pred[32]{0:T(512)(128)(4,1)}, pred[32]{0:T(512)(128)(4,1)S(1)}, u32[]{:S(2)}) copy-start(pred[32]{0:T(512)(128)(4,1)S(1)} %compare_and_fusion.1) | copy-start | bytes 100
  129.1 12.5 %all-to-all-start.4 = ((bf16[32,16,256]{2,1,0:T(8,128)(2,1)}), bf16[32,16,256]{2,1,0:T(8,128)(2,1)S(1)}, u32[]{:S(2)}, u32[]{:S(2)}) async-start(bf16[32,16,256]{2,1,0:T(8,128)(2,1)} %select_select_fusion.5), calls=%async_computation.4 | async-start | bytes 524288 | tf_op jit(solution)/shard_map/all_to_all | solution.py:98
  141.6 12.3 %all-to-all-start.2 = ((bf16[32,3,1024]{2,1,0:T(4,128)(2,1)}), bf16[32,3,1024]{2,1,0:T(4,128)(2,1)S(1)}, u32[]{:S(2)}, u32[]{:S(2)}) async-start(bf16[32,3,1024]{2,1,0:T(4,128)(2,1)} %select_select_fusion.3), calls=%async_computation.2 | async-start | bytes 524288 | tf_op jit(solution)/shard_map/all_to_all | solution.py:91
  147.8 62.5 %copy-start.15 = (bf16[8,16,1,2,128]{4,1,0,3,2:T(8,128)(2,1)}, bf16[8,16,1,2,128]{4,1,0,3,2:T(8,128)(2,1)S(1)}, u32[]{:S(2)}) copy-start(bf16[8,16,1,2,128]{4,1,0,3,2:T(8,128)(2,1)S(1)} %copy_select_fusion.1) | copy-start | bytes 196612
  153.8 57.0 %all-to-all-start.5 = ((bf16[32,17,256]{2,1,0:T(8,128)(2,1)}), bf16[32,17,256]{2,1,0:T(8,128)(2,1)S(1)}, u32[]{:S(2)}, u32[]{:S(2)}) async-start(bf16[32,17,256]{2,1,0:T(8,128)(2,1)} %select_select_fusion.2), calls=%async_computation.5 | async-start | bytes 786432 | tf_op jit(solution)/shard_map/all_to_all | solution.py:98
  159.1 144.8 %copy-start.19 = (s32[1024]{0:T(1024)S(1)}, s32[1024]{0:T(1024)}, u32[]{:S(2)}) copy-start(s32[1024]{0:T(1024)} %pad_clamp_fusion.4) | copy-start | bytes 12292
  211.6 195.8 %all-to-all-start.1 = ((f32[32,16,1024]{2,1,0:T(8,128)}), f32[32,16,1024]{2,1,0:T(8,128)S(1)}, u32[]{:S(2)}, u32[]{:S(2)}) async-start(f32[32,16,1024]{2,1,0:T(8,128)} %select_select_fusion.1), calls=%async_computation.1 | async-start | bytes 4194304 | tf_op jit(solution)/shard_map/all_to_all | solution.py:87
  221.2 82.6 %copy-start.12 = (bf16[8,17,1,2,128]{4,1,0,3,2:T(8,128)(2,1)}, bf16[8,17,1,2,128]{4,1,0,3,2:T(8,128)(2,1)S(1)}, u32[]{:S(2)}) copy-start(bf16[8,17,1,2,128]{4,1,0,3,2:T(8,128)(2,1)S(1)} %copy_select_fusion) | copy-start | bytes 208900
  222.2 83.6 %copy-start.23 = (f32[8,4,18]{2,1,0:T(4,128)}, f32[8,4,18]{2,1,0:T(4,128)S(1)}, u32[]{:S(2)}) copy-start(f32[8,4,18]{2,1,0:T(4,128)S(1)} %get-tuple-element.94) | copy-start | bytes 6916
  410.9 180.5 %all-to-all-start.3 = ((f32[32,16,1024]{2,1,0:T(8,128)}), f32[32,16,1024]{2,1,0:T(8,128)S(1)}, u32[]{:S(2)}, u32[]{:S(2)}) async-start(f32[32,16,1024]{2,1,0:T(8,128)} %select_select_fusion), calls=%async_computation.3 | async-start | bytes 4194304 | tf_op jit(solution)/shard_map/all_to_all | solution.py:87
  421.0 89.0 %reduce-scatter.7.cloned.1.call-start = ((), (), s32[]{:S(2)}) async-start(), calls=%async_computation.8 | async-start | bytes 139264
  433.5 158.6 %copy-start.21 = (f32[8,16]{1,0:T(8,128)S(1)}, f32[8,16]{1,0:T(8,128)}, u32[]{:S(2)}) copy-start(f32[8,16]{1,0:T(8,128)} %get-tuple-element.66) | copy-start | bytes 1540
  433.5 159.5 %copy-start.17 = (bf16[2,1,8,1024]{3,2,1,0:T(8,128)(2,1)S(1)}, bf16[2,1,8,1024]{3,2,1,0:T(8,128)(2,1)}, u32[]{:S(2)}) copy-start(bf16[2,1,8,1024]{3,2,1,0:T(8,128)(2,1)} %param.35) | copy-start | bytes 98308
  433.5 160.9 %copy-start.1 = (bf16[1024,288]{0,1:T(8,128)(2,1)S(1)}, bf16[1024,288]{0,1:T(8,128)(2,1)}, u32[]{:S(2)}) copy-start(bf16[1024,288]{0,1:T(8,128)(2,1)} %param.38) | copy-start | bytes 1769476
  433.5 156.5 %reduce-scatter.9.cloned.1.call-start = ((), (), s32[]{:S(2)}) async-start(), calls=%async_computation.9 | async-start | bytes 139264
  (37 other events, 464.1 us)
Sparse Core Ops, SparseCore 0:
  433.5 76.4 reduce-scatter.6
  513.9 76.1 reduce-scatter.8
where the time goes:
time: 608 us; the launch traced here: 602 us
  blocking collectives  221 us (36%)
  waiting for transfers between devices  149 us (25%)
  matrix products  70.2 us (12%)
  other arithmetic  56.7 us (9%)
  local copies, waits for them, and re-layouts  47.6 us (8%)
  starting transfers between devices  41.7 us (7%)
  between operations  15.5 us (3%)
    unnamed x4, waiting for transfers between devices  143 us
    pmax x1, blocking collectives, local(): highest = lax.pmax(local_top, 'beam')  79.1 us
    psum x1, blocking collectives, local(): normaliser = lax.psum(local_sum, 'beam')  69.8 us
    psum x1, blocking collectives, local(): projected = lax.psum(partial_value, 'tensor')  48.6 us
    dot_general x2, matrix products, local(): jnp.einsum('bpcgd,ptcd->bpcgt', page_queries, page_rows[:, :, :, 0], pref...  26.8 us
    dot_general x2, matrix products, local(): jnp.einsum('rp,bpcgd->brcgd', member_float, page_values, precision=lax.Pr...  23.7 us
    all_gather x1, blocking collectives, local(): all_queries = lax.all_gather(queries, 'beam', axis=1, tiled=True)  23.4 us
    all_to_all x2, starting transfers between devices, local(): lax.all_to_all(pack_slots(ssm_now, source_row, filled), 'beam', split_axi...  17.4 us
  transfers between devices with their start and end apart: 8, of which 4 were waited for; matrix products, arithmetic and copies ran while one was open for 27% of the time, Pallas kernels for 0%

commit v1 on v0

v1 whole, which is shorter than its diff:
```python
import jax
import jax.numpy as jnp
from jax import lax
from jax.experimental import pallas as pl
from jax.experimental.pallas import tpu as pltpu
from jax.sharding import PartitionSpec as P

NB = 16
REQ = 8
DS = 16
DT_RANK = 256
HD = 128
PAGE = 16
MAXP = 512
CH = 1024
LT = CH // 128
GROUP = 4
PAGES = 256
BLK = 16
NBLK = PAGES // BLK + REQ
UNROLL = 4
POOL = 4096
PROJ = DT_RANK + 2 * DS
PROJ_PAD = 384
LOG2E = 1.4426950408889634
NEG = -1e30

f32 = jnp.float32
bf16 = jnp.bfloat16
i32 = jnp.int32
MESH = pl.DeviceIdType.MESH


def iota(shape, dim):
    return lax.broadcasted_iota(i32, shape, dim)


def dot(a, b):
    return lax.dot_general(a, b, (((1,), (0,)), ((), ())), preferred_element_type=f32)


def dot_nt(a, b):
    return lax.dot_general(a, b, (((1,), (1,)), ((), ())), preferred_element_type=f32)


def one(mask):
    return jnp.where(mask, 1.0, 0.0).astype(bf16)


def onef(mask):
    return jnp.where(mask, 1.0, 0.0).astype(f32)


def to_rows(x):
    return jnp.concatenate([x[:, i * 128 : (i + 1) * 128] for i in range(LT)], axis=0)


def from_rows(x):
    return jnp.concatenate([x[i * REQ : (i + 1) * REQ] for i in range(LT)], axis=1)


def silu(v):
    return v / (1.0 + jnp.exp(-v))


def softplus(v):
    return jnp.maximum(v, 0.0) + jnp.log(1.0 + jnp.exp(-jnp.abs(v)))


def slot_key(par, me):
    chosen = par == me
    upper = one(iota((REQ, REQ), 0) < iota((REQ, REQ), 1))
    rank = dot(one(chosen), upper)
    return jnp.where(chosen, rank, -1.0)


def pack_matrix(key):
    rows, cols = NB * LT * 2, LT * REQ
    rb = one((iota((rows, NB), 0) >> 4) == iota((rows, NB), 1))
    cr = one((iota((REQ, cols), 1) & 7) == iota((REQ, cols), 0))
    spread = dot(dot(rb, key.astype(bf16)).astype(bf16), cr)
    row, col = iota((rows, cols), 0), iota((rows, cols), 1)
    return one((spread == (row & 1).astype(f32)) & (((row >> 1) & 7) == (col >> 3)))


def own_column(par, me):
    row = jnp.sum(jnp.where(iota((NB, REQ), 0) == me, par.astype(f32), 0.0), axis=0, keepdims=True)
    eye = iota((REQ, REQ), 0) == iota((REQ, REQ), 1)
    col = jnp.sum(jnp.where(eye, row, 0.0), axis=1, keepdims=True)
    return row, col


def unpack_matrix(par, me):
    row, col = own_column(par, me)
    alike = (row == col) & (iota((REQ, REQ), 1) < iota((REQ, REQ), 0))
    order = jnp.sum(onef(alike), axis=1, keepdims=True)
    code = jnp.concatenate([col * 2.0 + order] * LT, axis=0)
    rows, cols = LT * REQ, NB * LT * 2
    r, c = iota((rows, cols), 0), iota((rows, cols), 1)
    code_of = ((c >> 4) * 2 + (c & 1)).astype(f32)
    return one((code == code_of) & ((r >> 3) == ((c >> 1) & 7)))


def column128(m):
    spread = dot(one((iota((128, NB), 0) >> 3) == iota((128, NB), 1)), m.astype(bf16))
    pick = iota((128, REQ), 1) == (iota((128, REQ), 0) & 7)
    return jnp.sum(jnp.where(pick, spread, 0.0), axis=1, keepdims=True)


def kernel(
    par_h, po_h, ctx_h, cs_h, cw_h, cb_h, x_h, gate_h, q_h, nkv_h, suf_h, gain_h, dtb_h, rates_h, skip_h,
    s_h, xw_h, dtw_h, kv_h,
    mo_h, ao_h,
    par_ref, po_ref, ctx_ref, cs_ref, cw_ref, cb_ref, x_ref, gate_ref, q_ref, nkv_ref, suf_ref, gain_ref, dtb_ref,
    rates_ref, skip_ref, s_v, xw_v, dtw_v, kv_v,
    mo_ref, ao_ref,
    h1s, h1r, h2s, h2r, qa, zb, prb, zzs, zzr, os_, or_, lse,
    tab, tabs, bias, qr, orun, mrun, osf, s0, s1, rt, d1, d0g, c1, okm,
    lsem, tsem, ssem, rsem,
):
    me = lax.axis_index("beam")
    mt = lax.axis_index("tensor")
    nt = zb.shape[0]
    H1, H2, QA, ZB, PR, OO, LS, ZZ = range(8)

    def push(src, dst, to, k, axis):
        pltpu.make_async_remote_copy(
            src_ref=src, dst_ref=dst, send_sem=ssem.at[k], recv_sem=rsem.at[k], device_id={axis: to},
            device_id_type=MESH,
        ).start()

    def exchange(src, dst, k):
        for d in range(1, NB):
            peer = lax.rem(me + d, NB)
            push(src.at[peer], dst.at[me], peer, k, "beam")

    def gather(buf, k, n, my, axis):
        for d in range(1, n):
            push(buf.at[my], buf.at[my], lax.rem(my + d, n), k, axis)

    def all_of(buf, k, n, axis):
        part = buf.at[pl.ds(0, n - 1)]
        return pltpu.make_async_remote_copy(
            src_ref=part, dst_ref=part, send_sem=ssem.at[k], recv_sem=rsem.at[k], device_id={axis: 0},
            device_id_type=MESH,
        )

    def landed(buf, k, n=NB, axis="beam"):
        all_of(buf, k, n, axis).wait_recv()

    def sent(buf, k, n=NB, axis="beam"):
        all_of(buf, k, n, axis).wait_send()

    pairs = [
        (par_h, par_ref), (cs_h, cs_ref), (cw_h, cw_ref), (q_h, q_ref), (s_h, s_v), (rates_h, rates_ref),
        (x_h, x_ref), (cb_h, cb_ref), (po_h, po_ref), (ctx_h, ctx_ref), (xw_h, xw_v), (kv_h, kv_v),
        (suf_h, suf_ref), (nkv_h, nkv_ref), (dtw_h, dtw_v), (dtb_h, dtb_ref), (gain_h, gain_ref),
        (skip_h, skip_ref), (gate_h, gate_ref),
    ]
    copies = [pltpu.make_async_copy(a, b, lsem.at[i]) for i, (a, b) in enumerate(pairs)]
    (c_par, c_cs, c_cw, c_q, c_s, c_rates, c_x, c_cb, c_po, c_ctx, c_xw, c_kv, c_suf, c_nkv, c_dtw, c_dtb, c_gain,
     c_skip, c_gate) = copies
    for c in copies:
        c.start()
    barrier = pltpu.get_barrier_semaphore()
    for d in range(1, NB):
        pl.semaphore_signal(barrier, inc=1, device_id={"beam": lax.rem(me + d, NB)}, device_id_type=MESH)
    for d in range(1, nt):
        pl.semaphore_signal(barrier, inc=1, device_id={"tensor": lax.rem(mt + d, nt)}, device_id_type=MESH)

    c_par.wait()
    par_t = par_ref[...].astype(f32).astype(bf16)
    eye16 = one(iota((NB, NB), 0) == iota((NB, NB), 1))
    p0 = dot_nt(eye16, par_t[0:REQ]).astype(i32)
    p1 = dot_nt(eye16, par_t[REQ : 2 * REQ]).astype(i32)
    key0 = slot_key(p0, me)
    c_cs.wait()
    c_cw.wait()
    cw = cw_ref[...].astype(f32)
    cw_row = [cw[k : k + 1] for k in range(4)]
    win = [cs_ref[k].astype(f32) for k in range(3)]
    a0 = win[0] * cw_row[0] + win[1] * cw_row[1] + win[2] * cw_row[2]
    a1 = win[1] * cw_row[0] + win[2] * cw_row[1]
    both = jnp.concatenate([to_rows(a0), to_rows(a1)], axis=1).astype(bf16)
    packed = dot(pack_matrix(key0), both).astype(bf16)
    h1s[...] = packed.reshape(NB, 16, 256)
    h1r[pl.ds(me, 1)] = h1s[pl.ds(me, 1)]

    c_q.wait()
    qrows = jnp.concatenate(
        [q_ref[s][:, h * 128 : (h + 1) * 128].astype(f32) for s in range(2) for h in range(GROUP)], axis=0
    ).astype(bf16)
    ri, ci = iota((64, 64), 0), iota((64, 64), 1)
    swap = one(((ri >> 3) == (ci & 7)) & ((ri & 7) == (ci >> 3)))
    qa[pl.ds(me, 1)] = dot(swap, qrows).astype(bf16)[None]

    pl.semaphore_wait(barrier, NB - 1 + nt - 1)

    exchange(h1s, h1r, H1)

    key1 = slot_key(p1, me)
    pb1 = pack_matrix(key1)
    ub0 = unpack_matrix(p0, me)
    ub1 = unpack_matrix(p1, me)
    g = jnp.zeros((NB, REQ), i32)
    for p in range(NB):
        g = g + jnp.where(p1 == p, p0[p : p + 1, :], 0)
    wide = one((iota((REQ, REQ * 128), 1) >> 7) == iota((REQ, REQ * 128), 0))
    x_s0 = dot(one(p0 == me), wide)
    x_sg = dot(one(g == me), wide)
    x_s1 = dot(one(p1 == me), wide)
    tok = iota((NB, REQ * 128), 1) & 127
    mine = onef(iota((NB, REQ * 128), 0) == me)
    ok0 = jnp.where(tok < 16, x_s0, jnp.where(tok == 16, mine, 0.0))
    ok1 = jnp.where(tok < 16, x_sg, jnp.where(tok == 16, x_s1, jnp.where(tok == 17, mine, 0.0)))
    qi, qj = iota((128, 2 * NB), 0), iota((128, 2 * NB), 1)
    pick = one((((qi >> 2) & 1) == (qj >> 4)) & ((qi >> 3) == (qj & 15)))
    okm[...] = dot(pick, jnp.concatenate([ok0, ok1], axis=0).astype(bf16))

    c_rates.wait()
    for n in range(DS):
        rt[n] = jnp.broadcast_to(rates_ref[n : n + 1, :] * (-LOG2E), (REQ, CH))
    c_s.wait()
    row, col = iota((DS * NB * 2, 128), 0), iota((DS * NB * 2, 128), 1)
    rs_ = one(((iota((DS * NB * 2, NB), 0) >> 1) & 15) == iota((DS * NB * 2, NB), 1))
    crn = one((iota((REQ, 128), 1) >> 4) == iota((REQ, 128), 0))
    keys = dot(rs_, dot(key0.astype(bf16), crn).astype(bf16))
    sel0 = one((keys == (row & 1).astype(f32)) & ((row >> 5) == (col & 15)))
    pi, pj = iota((128, 128), 0), iota((128, 128), 1)
    perm1 = one(((pi & 7) == (pj >> 4)) & ((pi >> 3) == (pj & 15)))
    for j in range(4):
        sl = slice(j * 256, (j + 1) * 256)
        sj = s_v[:, sl].astype(bf16)
        s0[:, :, sl] = dot(sel0, sj).reshape(DS, NB * 2, 256)
        s1[:, :, sl] = dot(perm1, sj).reshape(DS, REQ, 256)

    c_x.wait()
    c_cb.wait()
    x0 = x_ref[0].astype(f32)
    x1 = x_ref[1].astype(f32)
    cb8 = cb_ref[...].astype(f32)
    cb = jnp.concatenate([cb8[i : i + 1] for i in range(LT)], axis=1)

    landed(h1r, H1)
    got = dot(ub0, h1r[...].reshape(NB * 16, 256))
    c0 = from_rows(got[:, 0:128]) + cw_row[3] * x0 + cb
    w1 = from_rows(got[:, 128:256]) + cw_row[2] * x0
    both = jnp.concatenate([to_rows(c0), to_rows(w1)], axis=1).astype(bf16)
    h2s[...] = dot(pb1, both).astype(bf16).reshape(NB, 16, 256)
    h2r[pl.ds(me, 1)] = h2s[pl.ds(me, 1)]
    exchange(h2s, h2r, H2)
    gather(qa, QA, NB, me, "beam")

    c_po.wait()
    c_ctx.wait()
    ctx_col = jnp.zeros((REQ, MAXP), i32)
    for r in range(REQ):
        ctx_col = jnp.where(iota((REQ, MAXP), 0) == r, ctx_ref[r], ctx_col)
    nvis = jnp.clip(ctx_col - iota((REQ, MAXP), 1) * PAGE, 0, PAGE)
    po = jnp.concatenate([po_ref[pl.ds(j, REQ, stride=4), :] for j in range(4)], axis=1)
    loc = po - me * PAGES
    flag = (loc >= 0) & (loc < PAGES) & (nvis > 0)
    tri = one(iota((MAXP, MAXP), 0) < iota((MAXP, MAXP), 1))
    rank = dot(one(flag), tri).astype(i32)
    count = jnp.sum(onef(flag), axis=1, keepdims=True).astype(i32)
    nblk = ((count + (BLK - 1)) >> 4).astype(f32)
    eye8 = iota((REQ, REQ), 0) == iota((REQ, REQ), 1)
    nblk_row = jnp.sum(jnp.where(eye8, nblk, 0.0), axis=0, keepdims=True)
    sblk = jnp.sum(
        jnp.where(iota((REQ, REQ), 1) < iota((REQ, REQ), 0), nblk_row, 0.0), axis=1, keepdims=True
    )
    dest = jnp.where(flag, sblk.astype(i32) * BLK + rank, -1)
    hi = dest >> 4
    lo = jnp.where(flag, dest & 15, -1)
    table = jnp.zeros((NBLK, 32), f32)
    for r in range(REQ):
        hot = one(hi[r : r + 1] == iota((NBLK, MAXP), 0))
        low = lo[r : r + 1] == iota((16, MAXP), 0)
        vals = jnp.concatenate(
            [
                jnp.where(low, loc[r : r + 1].astype(f32), 0.0),
                jnp.where(low, nvis[r : r + 1].astype(f32), 0.0),
            ],
            axis=0,
        ).astype(bf16)
        table = table + dot_nt(hot, vals)
    tab[...] = jnp.zeros_like(tab)
    tab[0:NBLK, 0:32] = table.astype(i32)
    lane = iota((REQ, 128), 1)
    subl = iota((REQ, 128), 0)
    sb_i, nb_i = sblk.astype(i32), nblk.astype(i32)
    inside = (sb_i <= lane) & (lane < sb_i + nb_i)
    tab[NBLK : NBLK + 1, :] = jnp.sum(jnp.where(inside, subl, 0).astype(f32), axis=0, keepdims=True).astype(i32)
    tab[NBLK + 1 : NBLK + 2, :] = jnp.sum(
        onef((lane == sb_i) & (nb_i > 0)), axis=0, keepdims=True
    ).astype(i32)
    tab[NBLK + 2 : NBLK + 3, :] = jnp.sum(
        jnp.where((lane == subl) & (nb_i > 0), sb_i + nb_i, 0).astype(f32), axis=0, keepdims=True
    ).astype(i32)
    cp_tab = pltpu.make_async_copy(tab, tabs, tsem)
    cp_tab.start()
    spread = one((iota((16, BLK * PAGE), 1) >> 4) == iota((16, BLK * PAGE), 0))
    seen = dot(table[:, 16:32].astype(bf16), spread)
    bias[...] = jnp.where((iota((NBLK, BLK * PAGE), 1) & 15).astype(f32) < seen, 0.0, NEG)
    orun[0] = jnp.zeros((128, 2 * HD), f32)
    mrun[0] = jnp.full((128, HD), NEG, f32)
    cp_tab.wait()

    c_xw.wait()
    landed(h2r, H2)
    got = dot(ub1, h2r[...].reshape(NB * 16, 256))
    conv0p = silu(from_rows(got[:, 0:128]))
    conv0 = silu(c0)
    conv1 = silu(from_rows(got[:, 128:256]) + cw_row[3] * x1 + cb)
    part = dot_nt(jnp.concatenate([conv0, conv1], axis=0).astype(bf16), xw_v[...])
    zb[pl.ds(mt, 1)] = jnp.zeros((1, 16, PROJ_PAD), bf16)
    zb[pl.ds(mt, 1), :, 0:PROJ] = part.astype(bf16)[None]
    gather(zb, ZB, nt, mt, "tensor")

    landed(qa, QA)
    qf = qa[...].astype(f32)
    for r in range(REQ):
        qr[r] = jnp.concatenate([qf[b, r * 8 : (r + 1) * 8] for b in range(NB)], axis=0).astype(bf16)
    c_kv.wait()
    scale = HD**-0.5 * LOG2E
    ones_blk = jnp.ones((BLK * PAGE, HD), bf16)

    def blocks(step, c):
        first = step * UNROLL
        m_old, o_old = mrun[first], orun[first]
        for u in range(UNROLL):
            i = first + u
            kv = jnp.concatenate([kv_v[tabs[i, k] & (PAGES - 1)] for k in range(BLK)], axis=0)
            s = dot_nt(qr[tabs[NBLK, i] & (REQ - 1)], kv[:, 0:HD]) * scale + bias[pl.ds(i, 1), :]
            m_old = jnp.where(tabs[NBLK + 1, i] > 0, NEG, m_old)
            m_new = jnp.maximum(m_old, jnp.max(s, axis=1, keepdims=True))
            e = jnp.exp2(s - jnp.concatenate([m_new, m_new], axis=1)).astype(bf16)
            v = jnp.concatenate([kv[:, HD : 2 * HD], ones_blk], axis=1)
            fade = jnp.exp2(m_old - m_new)
            o_old = o_old * jnp.concatenate([fade, fade], axis=1) + dot(e, v)
            m_old = m_new
            orun[i + 1] = o_old
            mrun[i + 1] = m_old
        return c

    steps = NBLK // UNROLL
    lax.fori_loop(0, steps // 2, blocks, 0)

    landed(zb, ZB, nt, "tensor")
    proj = jnp.zeros((16, PROJ_PAD), f32)
    for t in range(nt):
        proj = proj + zb[t].astype(f32)
    prb[pl.ds(me, 1)] = proj.astype(bf16)[None]
    gather(prb, PR, NB, me, "beam")

    lax.fori_loop(steps // 2, steps, blocks, 0)
    c_suf.wait()
    c_nkv.wait()
    nk0 = nkv_ref[0].astype(f32)
    nk1 = nkv_ref[1].astype(f32)
    diag = iota((128, 128), 0) == iota((128, 128), 1)
    ti = iota((16, 256), 0)
    for r in range(REQ):
        tail = jnp.where(ti == 0, nk0[r : r + 1], jnp.where(ti == 1, nk1[r : r + 1], 0.0)).astype(bf16)
        kv = jnp.concatenate([suf_ref[r], tail], axis=0)
        s = jnp.where(
            okm[:, r * 128 : r * 128 + 32] > 0.5, dot_nt(qr[r], kv[:, 0:HD]) * scale, NEG
        )
        last = jnp.clip(tabs[NBLK + 2, r], 0, NBLK)
        m_old = mrun[last]
        m_new = jnp.maximum(m_old, jnp.max(s, axis=1, keepdims=True))
        e = jnp.exp2(s - m_new[:, 0:32]).astype(bf16)
        v = jnp.concatenate([kv[:, HD : 2 * HD], jnp.ones((32, HD), bf16)], axis=1)
        fade = jnp.exp2(m_old - m_new)
        o = orun[last] * jnp.concatenate([fade, fade], axis=1) + dot(e, v)
        total = o[:, HD : 2 * HD]
        val = o[:, 0:HD] / total
        for b in range(NB):
            osf[b, r * 8 : (r + 1) * 8, :] = val[b * 8 : (b + 1) * 8]
        lg = m_new + jnp.log2(total)
        lse[pl.ds(me, 1), r : r + 1, :] = jnp.sum(jnp.where(diag, lg, 0.0), axis=0, keepdims=True)[None]
    os_[...] = osf[...].astype(bf16)
    or_[pl.ds(me, 1)] = os_[pl.ds(me, 1)]
    exchange(os_, or_, OO)
    gather(lse, LS, NB, me, "beam")

    for c in (c_dtw, c_dtb, c_gain, c_skip, c_gate):
        c.wait()
    gain = gain_ref[...]

    def normed(rank_rows):
        mean = jnp.sum(rank_rows * rank_rows, axis=1, keepdims=True) * (1.0 / DT_RANK)
        return (rank_rows * lax.rsqrt(mean + 1e-6) * gain).astype(bf16)

    dtb = dtb_ref[...]
    own = proj.astype(bf16).astype(f32)
    d_own = softplus(dot(normed(own[:, 0:DT_RANK]), dtw_v[...]) + dtb)
    d_own0, d_own1 = d_own[0:REQ], d_own[REQ : 2 * REQ]
    own_in = own[:, DT_RANK : DT_RANK + DS]
    own_out = own[:, DT_RANK + DS : DT_RANK + 2 * DS]
    cb_own = jnp.sum(own_in * own_out, axis=1, keepdims=True)
    skip = skip_ref[...]
    base0 = d_own0 * conv0 * cb_own[0:REQ] + skip * conv0
    base1 = d_own1 * conv1 * cb_own[REQ : 2 * REQ] + skip * conv1
    gate0 = silu(gate_ref[0].astype(f32))
    gate1 = silu(gate_ref[1].astype(f32))

    landed(prb, PR)
    prf = prb[...].astype(f32)
    pr0 = prf[:, 0:REQ, :].reshape(128, PROJ_PAD)
    pr1 = prf[:, REQ : 2 * REQ, :].reshape(128, PROJ_PAD)
    rn0 = normed(pr0[:, 0:DT_RANK])
    rn1 = normed(pr1[:, 0:DT_RANK])
    bc0 = pr0[:, DT_RANK:PROJ].astype(bf16)
    c1[...] = (pr1[:, DT_RANK:PROJ_PAD] * column128(onef(g == me))).reshape(NB, REQ, 128)
    g1 = one((column128(p1) == (pj >> 3).astype(f32)) & ((pi & 7) == (pj & 7)))
    rn0g = dot(g1, rn0).astype(bf16)

    r32 = one((iota((32, NB), 0) >> 1) == iota((32, NB), 1))
    c32 = one((iota((REQ, 128), 1) & 7) == iota((REQ, 128), 0))
    key32 = dot(dot(r32, key0.astype(bf16)).astype(bf16), c32)
    si, sj_ = iota((32, 128), 0), iota((32, 128), 1)
    psl = one((key32 == (si & 1).astype(f32)) & ((si >> 1) == (sj_ >> 3)))
    rn0s = dot(psl, rn0).astype(bf16)
    c0s = dot(psl, bc0)
    c0b = [jnp.broadcast_to(c0s[:, DS + n : DS + n + 1], (NB * 2, 128)) for n in range(DS)]
    z0 = []
    for j in range(4):
        sl = slice(j * 256, (j + 1) * 256)
        w = dtw_v[:, sl]
        part1 = softplus(dot(rn1, w) + dtb[:, sl])
        part0 = softplus(dot(rn0g, w) + dtb[:, sl])
        d0g[:, :, sl] = part0.reshape(NB, REQ, 256)
        d1[:, :, sl] = (part0 + part1).reshape(NB, REQ, 256)
        dj = softplus(dot(rn0s, w) + dtb[:, sl])
        acc = jnp.zeros((32, 256), f32)
        for n in range(DS):
            cn = jnp.concatenate([c0b[n], c0b[n]], axis=1)
            acc = acc + cn * (jnp.exp2(dj * (rates_ref[n : n + 1, sl] * (-LOG2E))) * s0[n, :, sl])
        z0 += [acc[:, 0:128], acc[:, 128:256]]
    z0 = jnp.concatenate(z0, axis=0).astype(bf16)
    ui, uj = iota((256, 256), 0), iota((256, 256), 1)
    relay = one(((ui >> 4) == ((uj >> 1) & 15)) & (((ui >> 1) & 7) == (uj >> 5)) & ((ui & 1) == (uj & 1)))
    zzs[:, 64:80, :] = dot(relay, z0).astype(bf16).reshape(NB, 16, 128)

    def children(i, c):
        two = [lax.rem(me + 1 + 2 * i, NB), lax.rem(me + 2 + 2 * i, NB)]
        outs = [c1[b] for b in two]
        deltas = [d1[b] for b in two]
        accs = [jnp.zeros((REQ, CH), f32) for _ in two]
        for n in range(DS):
            rn, sn = rt[n], s1[n]
            for k in range(2):
                accs[k] = accs[k] + outs[k][:, DS + n : DS + n + 1] * (jnp.exp2(deltas[k] * rn) * sn)
        for k in range(2):
            zzs[two[k], 0:64, :] = to_rows(accs[k]).astype(bf16)
        push(zzs.at[two[0]], zzr.at[me], two[0], ZZ, "beam")

        @pl.when(i < NB // 2 - 1)
        def _():
            push(zzs.at[two[1]], zzr.at[me], two[1], ZZ, "beam")

        return c

    lax.fori_loop(0, NB // 2, children, 0)
    zzr[pl.ds(me, 1)] = zzs[pl.ds(me, 1)]

    _, own1 = own_column(p1, me)
    gi, gj = iota((REQ, 128), 0), iota((REQ, 128), 1)
    og = one((own1 == (gj >> 3).astype(f32)) & (gi == (gj & 7)))
    in0p = dot(og, bc0)[:, 0:DS]
    cross = in0p * own_out[REQ : 2 * REQ]
    mixed = jnp.zeros((REQ, CH), f32)
    for n in range(DS):
        mixed = mixed + cross[:, n : n + 1] * jnp.exp2(d_own1 * rt[n])
    base1 = base1 + mixed * (d0g[pl.ds(me, 1)][0] * conv0p)

    landed(or_, OO)
    landed(lse, LS)
    lanes = iota((8, 128), 1)
    want = lanes == me * 8 + iota((8, 128), 0)
    parts = []
    for p in range(NB):
        lp = lse[p]
        parts.append(
            jnp.concatenate(
                [
                    jnp.sum(jnp.where(want, lp[r : r + 1], 0.0), axis=1, keepdims=True)
                    for r in range(REQ)
                ],
                axis=0,
            )
        )
    top = parts[0]
    for p in range(1, NB):
        top = jnp.maximum(top, parts[p])
    den = jnp.zeros((64, 1), f32)
    num = jnp.zeros((64, HD), f32)
    for p in range(NB):
        w = jnp.exp2(parts[p] - top)
        den = den + w
        num = num + w * or_[p].astype(f32)
    att = dot(swap, (num / den).astype(bf16))
    for s in range(2):
        ao_ref[s, 0] = jnp.concatenate(
            [att[(s * GROUP + h) * 8 : (s * GROUP + h + 1) * 8] for h in range(GROUP)], axis=1
        ).astype(bf16)
    out_a = pltpu.make_async_copy(ao_ref, ao_h, tsem)
    out_a.start()

    landed(zzr, ZZ)
    z1 = jnp.zeros((64, 128), f32)
    for p in range(NB):
        z1 = z1 + zzr[p, 0:64, :].astype(f32)
    z0 = dot(ub0, zzr[:, 64:80, :].reshape(256, 128))
    mo_ref[0, 0] = ((from_rows(z0) + base0) * gate0).astype(bf16)
    mo_ref[1, 0] = ((from_rows(z1) + base1) * gate1).astype(bf16)
    out_m = pltpu.make_async_copy(mo_ref, mo_h, lsem.at[0])
    out_m.start()

    sent(h1s, H1)
    sent(h2s, H2)
    sent(qa, QA)
    sent(zb, ZB, nt, "tensor")
    sent(prb, PR)
    sent(os_, OO)
    sent(lse, LS)
    sent(zzs, ZZ)
    out_a.wait()
    out_m.wait()


def local(
    ssm_state,
    conv_state,
    suffix_kv,
    mamba_x,
    mamba_gate,
    conv_weight,
    conv_bias,
    xproj_weight,
    dt_gain,
    dtproj_weight,
    dt_bias,
    state_rates,
    skip_gain,
    queries,
    new_kv,
    kv_pool,
    page_order,
    ctx_len,
    parents,
):
    nt = lax.axis_size("tensor")
    hb = pl.BlockSpec(memory_space=pltpu.HBM)
    dma = pltpu.SemaphoreType.DMA
    V = pltpu.VMEM
    operands = [
        parents.transpose(0, 2, 1, 3).reshape(2 * REQ, NB),
        page_order.reshape(POOL // 128, 128),
        ctx_len,
        conv_state.transpose(0, 2, 1, 3)[0],
        conv_weight,
        conv_bias.reshape(LT, 128),
        mamba_x[:, 0],
        mamba_gate[:, 0],
        queries[:, 0],
        new_kv[:, 0],
        suffix_kv[0],
        dt_gain.reshape(1, DT_RANK),
        dt_bias.reshape(1, CH),
        state_rates,
        skip_gain.reshape(1, CH),
        ssm_state.reshape(REQ * DS, CH),
        xproj_weight.T,
        dtproj_weight,
        kv_pool,
    ]
    held = [V(a.shape, a.dtype) for a in operands]
    held[2] = pltpu.SMEM((REQ,), i32)
    outs = (
        jax.ShapeDtypeStruct((2, 1, REQ, CH), bf16),
        jax.ShapeDtypeStruct((2, 1, REQ, GROUP * HD), bf16),
    )
    return pl.pallas_call(
        kernel,
        out_shape=outs,
        in_specs=[hb] * len(operands),
        out_specs=(hb, hb),
        scratch_shapes=held
        + [
            V(outs[0].shape, bf16),
            V(outs[1].shape, bf16),
            V((NB, 16, 256), bf16),
            V((NB, 16, 256), bf16),
            V((NB, 16, 256), bf16),
            V((NB, 16, 256), bf16),
            V((NB, 64, HD), bf16),
            V((nt, 16, PROJ_PAD), bf16),
            V((NB, 16, PROJ_PAD), bf16),
            V((NB, 80, 128), bf16),
            V((NB, 80, 128), bf16),
            V((NB, 64, HD), bf16),
            V((NB, 64, HD), bf16),
            V((NB, REQ, 128), f32),
            V((32, 128), i32),
            pltpu.SMEM((32, 128), i32),
            V((NBLK, BLK * PAGE), f32),
            V((REQ, 128, HD), bf16),
            V((NBLK + 1, 128, 2 * HD), f32),
            V((NBLK + 1, 128, HD), f32),
            V((NB, 64, HD), f32),
            V((DS, NB * 2, CH), f32),
            V((DS, REQ, CH), f32),
            V((DS, REQ, CH), f32),
            V((NB, REQ, CH), f32),
            V((NB, REQ, CH), f32),
            V((NB, REQ, 128), f32),
            V((128, REQ * 128), f32),
            dma((len(operands),)),
            dma,
            dma((8,)),
            dma((8,)),
        ],
        compiler_params=pltpu.CompilerParams(
            collective_id=0, has_side_effects=True, vmem_limit_bytes=63 * 2**20
        ),
        name="decode",
    )(*operands)


def solution(mesh):
    in_specs = (
        P("beam", None, None, "tensor"),
        P("beam", None, None, "tensor"),
        P("beam", None, None, "tensor"),
        P(None, "beam", None, "tensor"),
        P(None, "beam", None, "tensor"),
        P(None, "tensor"),
        P("tensor"),
        P("tensor", None),
        P(),
        P(None, "tensor"),
        P("tensor"),
        P(None, "tensor"),
        P("tensor"),
        P(None, "beam", None, "tensor"),
        P(None, "beam", None, "tensor"),
        P("beam", None, "tensor"),
        P(),
        P(),
        P(),
    )
    out_specs = (P(None, "beam", None, "tensor"), P(None, "beam", None, "tensor"))
    return jax.shard_map(local, mesh=mesh, in_specs=in_specs, out_specs=out_specs, check_vma=False)
```

time: 608 us -> 45.6 us (0.07)
  blocking collectives: 221 us -> 0 us
  waiting for transfers between devices: 149 us -> 0 us
  matrix products: 70.2 us -> 0 us
  other arithmetic: 56.7 us -> 0 us
  local copies, waits for them, and re-layouts: 47.6 us -> 2.7 us
  starting transfers between devices: 41.7 us -> 0 us
  Pallas kernels: 0 us -> 41.5 us
  between operations: 15.5 us -> 0.65 us
    unnamed x4 -> x0, waiting for transfers between devices: 143 us -> none
    psum x2 -> x0, blocking collectives: 118 us -> none  [the longest x1 69.8 us: local(): normaliser = lax.psum(local_sum, 'beam')]
    pmax x1 -> x0, blocking collectives: 79.1 us -> none  [local(): highest = lax.pmax(local_top, 'beam')]
    dot_general x16 -> x0, matrix products: 70.2 us -> none  [the longest x2 26.8 us: local(): jnp.einsum('bpcgd,ptcd->bpcgt', page_queries, page_rows[:, :, :, 0], pref...]
    pallas_call x0 -> x1, Pallas kernels: none -> 41.5 us  [local(): pl.pallas_call(kernel, out_shape=outs, in_specs=[hb] * len(operands), out...]
    all_to_all x6 -> x0, starting transfers between devices: 41.1 us -> none  [the longest x2 17.4 us: local(): lax.all_to_all(pack_slots(ssm_now, source_row, filled), 'beam', split_axi...]
    all_gather x1 -> x0, blocking collectives: 23.4 us -> none  [local(): all_queries = lax.all_gather(queries, 'beam', axis=1, tiled=True)]
    gather x21 -> x0, local copies, waits for them, and re-layouts: 22.7 us -> none  [the longest x2 5.54 us: local(): jnp.take(all_queries[decode_step], page_request, axis=1)]
  transfers between devices with their start and end apart: 8 -> 0, of which waited for: 4 -> 0; matrix products, arithmetic and copies ran while one was open for 27% -> 0% of each run, Pallas kernels for 0% -> 0%
where the time goes in v1:
time: 45.6 us; the launch traced here: 44.8 us
  Pallas kernels  41.5 us (91%)
  local copies, waits for them, and re-layouts  2.7 us (6%)
  between operations  0.65 us (1%)
    pallas_call x1, Pallas kernels, local(): pl.pallas_call(kernel, out_shape=outs, in_specs=[hb] * len(operands), out...  41.5 us
    unnamed x2, local copies, waits for them, and re-layouts  2.7 us

profile of v1, /device:TPU:2, one launch (start us, length us, event | category | flops | bytes accessed | tf_op | source)
XLA Modules:
  0.0 44.8 jit_solution(12973978899262266413)
XLA Ops:
  0.6 41.5 %decode.1 = (bf16[2,1,8,1024]{3,2,1,0:T(8,128)(2,1)}, bf16[2,1,8,512]{3,2,1,0:T(8,128)(2,1)}) custom-call(s32[16,16]{1,0:T(8,128)} %bitcast.26, s32[32,128]{1,0:T(8,128)} %bitcast.24, s32[8]{0:T(128)} %ctx_h.1, bf16[3,8,1024]{2,1,0:T(8,128)(2,1)} %bitcast.21, bf16[4,1024]{1,0:T(4,128)(2,1)} %cw_h.1, bf16[8,128]{1,0:T(8,128)(2,1)} %bitcast.30, ...), custom_call_target="tpu_custom_call" | custom-call | tf_op jit(solution)/shard_map/decode/pallas_call | solution.py:585
  42.1 1.4 %copy.23 = bf16[2,1,8,1024]{3,2,1,0:T(8,128)(2,1)} copy(bf16[2,1,8,1024]{3,2,1,0:T(8,128)(2,1)} %get-tuple-element.4) | data formatting | bytes 65536
  43.5 1.3 %copy.24 = bf16[2,1,8,512]{3,2,1,0:T(8,128)(2,1)} copy(bf16[2,1,8,512]{3,2,1,0:T(8,128)(2,1)} %get-tuple-element.5) | data formatting | bytes 32768

commit v2 on v1

--- a/solution.py
+++ b/solution.py
@@ -18,7 +18,7 @@
 PAGES = 256
 BLK = 16
 NBLK = PAGES // BLK + REQ
-UNROLL = 4
+UNROLL = 8
 POOL = 4096
 PROJ = DT_RANK + 2 * DS
 PROJ_PAD = 384
@@ -197,6 +197,7 @@
     pl.semaphore_wait(barrier, NB - 1 + nt - 1)
 
     exchange(h1s, h1r, H1)
+    gather(qa, QA, NB, me, "beam")
 
     key1 = slot_key(p1, me)
     pb1 = pack_matrix(key1)
@@ -205,52 +206,6 @@
     g = jnp.zeros((NB, REQ), i32)
     for p in range(NB):
         g = g + jnp.where(p1 == p, p0[p : p + 1, :], 0)
-    wide = one((iota((REQ, REQ * 128), 1) >> 7) == iota((REQ, REQ * 128), 0))
-    x_s0 = dot(one(p0 == me), wide)
-    x_sg = dot(one(g == me), wide)
-    x_s1 = dot(one(p1 == me), wide)
-    tok = iota((NB, REQ * 128), 1) & 127
-    mine = onef(iota((NB, REQ * 128), 0) == me)
-    ok0 = jnp.where(tok < 16, x_s0, jnp.where(tok == 16, mine, 0.0))
-    ok1 = jnp.where(tok < 16, x_sg, jnp.where(tok == 16, x_s1, jnp.where(tok == 17, mine, 0.0)))
-    qi, qj = iota((128, 2 * NB), 0), iota((128, 2 * NB), 1)
-    pick = one((((qi >> 2) & 1) == (qj >> 4)) & ((qi >> 3) == (qj & 15)))
-    okm[...] = dot(pick, jnp.concatenate([ok0, ok1], axis=0).astype(bf16))
-
-    c_rates.wait()
-    for n in range(DS):
-        rt[n] = jnp.broadcast_to(rates_ref[n : n + 1, :] * (-LOG2E), (REQ, CH))
-    c_s.wait()
-    row, col = iota((DS * NB * 2, 128), 0), iota((DS * NB * 2, 128), 1)
-    rs_ = one(((iota((DS * NB * 2, NB), 0) >> 1) & 15) == iota((DS * NB * 2, NB), 1))
-    crn = one((iota((REQ, 128), 1) >> 4) == iota((REQ, 128), 0))
-    keys = dot(rs_, dot(key0.astype(bf16), crn).astype(bf16))
-    sel0 = one((keys == (row & 1).astype(f32)) & ((row >> 5) == (col & 15)))
-    pi, pj = iota((128, 128), 0), iota((128, 128), 1)
-    perm1 = one(((pi & 7) == (pj >> 4)) & ((pi >> 3) == (pj & 15)))
-    for j in range(4):
-        sl = slice(j * 256, (j + 1) * 256)
-        sj = s_v[:, sl].astype(bf16)
-        s0[:, :, sl] = dot(sel0, sj).reshape(DS, NB * 2, 256)
-        s1[:, :, sl] = dot(perm1, sj).reshape(DS, REQ, 256)
-
-    c_x.wait()
-    c_cb.wait()
-    x0 = x_ref[0].astype(f32)
-    x1 = x_ref[1].astype(f32)
-    cb8 = cb_ref[...].astype(f32)
-    cb = jnp.concatenate([cb8[i : i + 1] for i in range(LT)], axis=1)
-
-    landed(h1r, H1)
-    got = dot(ub0, h1r[...].reshape(NB * 16, 256))
-    c0 = from_rows(got[:, 0:128]) + cw_row[3] * x0 + cb
-    w1 = from_rows(got[:, 128:256]) + cw_row[2] * x0
-    both = jnp.concatenate([to_rows(c0), to_rows(w1)], axis=1).astype(bf16)
-    h2s[...] = dot(pb1, both).astype(bf16).reshape(NB, 16, 256)
-    h2r[pl.ds(me, 1)] = h2s[pl.ds(me, 1)]
-    exchange(h2s, h2r, H2)
-    gather(qa, QA, NB, me, "beam")
-
     c_po.wait()
     c_ctx.wait()
     ctx_col = jnp.zeros((REQ, MAXP), i32)
@@ -306,16 +261,21 @@
     mrun[0] = jnp.full((128, HD), NEG, f32)
     cp_tab.wait()
 
-    c_xw.wait()
-    landed(h2r, H2)
-    got = dot(ub1, h2r[...].reshape(NB * 16, 256))
-    conv0p = silu(from_rows(got[:, 0:128]))
-    conv0 = silu(c0)
-    conv1 = silu(from_rows(got[:, 128:256]) + cw_row[3] * x1 + cb)
-    part = dot_nt(jnp.concatenate([conv0, conv1], axis=0).astype(bf16), xw_v[...])
-    zb[pl.ds(mt, 1)] = jnp.zeros((1, 16, PROJ_PAD), bf16)
-    zb[pl.ds(mt, 1), :, 0:PROJ] = part.astype(bf16)[None]
-    gather(zb, ZB, nt, mt, "tensor")
+    c_x.wait()
+    c_cb.wait()
+    x0 = x_ref[0].astype(f32)
+    x1 = x_ref[1].astype(f32)
+    cb8 = cb_ref[...].astype(f32)
+    cb = jnp.concatenate([cb8[i : i + 1] for i in range(LT)], axis=1)
+
+    landed(h1r, H1)
+    got = dot(ub0, h1r[...].reshape(NB * 16, 256))
+    c0 = from_rows(got[:, 0:128]) + cw_row[3] * x0 + cb
+    w1 = from_rows(got[:, 128:256]) + cw_row[2] * x0
+    both = jnp.concatenate([to_rows(c0), to_rows(w1)], axis=1).astype(bf16)
+    h2s[...] = dot(pb1, both).astype(bf16).reshape(NB, 16, 256)
+    h2r[pl.ds(me, 1)] = h2s[pl.ds(me, 1)]
+    exchange(h2s, h2r, H2)
 
     landed(qa, QA)
     qf = qa[...].astype(f32)
@@ -344,7 +304,50 @@
         return c
 
     steps = NBLK // UNROLL
-    lax.fori_loop(0, steps // 2, blocks, 0)
+    lax.fori_loop(0, 1, blocks, 0)
+
+    c_xw.wait()
+    landed(h2r, H2)
+    got = dot(ub1, h2r[...].reshape(NB * 16, 256))
+    conv0p = silu(from_rows(got[:, 0:128]))
+    conv0 = silu(c0)
+    conv1 = silu(from_rows(got[:, 128:256]) + cw_row[3] * x1 + cb)
+    part = dot_nt(jnp.concatenate([conv0, conv1], axis=0).astype(bf16), xw_v[...])
+    zb[pl.ds(mt, 1)] = jnp.zeros((1, 16, PROJ_PAD), bf16)
+    zb[pl.ds(mt, 1), :, 0:PROJ] = part.astype(bf16)[None]
+    gather(zb, ZB, nt, mt, "tensor")
+
+
+    wide = one((iota((REQ, REQ * 128), 1) >> 7) == iota((REQ, REQ * 128), 0))
+    x_s0 = dot(one(p0 == me), wide)
+    x_sg = dot(one(g == me), wide)
+    x_s1 = dot(one(p1 == me), wide)
+    tok = iota((NB, REQ * 128), 1) & 127
+    mine = onef(iota((NB, REQ * 128), 0) == me)
+    ok0 = jnp.where(tok < 16, x_s0, jnp.where(tok == 16, mine, 0.0))
+    ok1 = jnp.where(tok < 16, x_sg, jnp.where(tok == 16, x_s1, jnp.where(tok == 17, mine, 0.0)))
+    qi, qj = iota((128, 2 * NB), 0), iota((128, 2 * NB), 1)
+    pick = one((((qi >> 2) & 1) == (qj >> 4)) & ((qi >> 3) == (qj & 15)))
+    okm[...] = dot(pick, jnp.concatenate([ok0, ok1], axis=0).astype(bf16))
+
+    c_rates.wait()
+    for n in range(DS):
+        rt[n] = jnp.broadcast_to(rates_ref[n : n + 1, :] * (-LOG2E), (REQ, CH))
+    c_s.wait()
+    row, col = iota((DS * NB * 2, 128), 0), iota((DS * NB * 2, 128), 1)
+    rs_ = one(((iota((DS * NB * 2, NB), 0) >> 1) & 15) == iota((DS * NB * 2, NB), 1))
+    crn = one((iota((REQ, 128), 1) >> 4) == iota((REQ, 128), 0))
+    keys = dot(rs_, dot(key0.astype(bf16), crn).astype(bf16))
+    sel0 = one((keys == (row & 1).astype(f32)) & ((row >> 5) == (col & 15)))
+    pi, pj = iota((128, 128), 0), iota((128, 128), 1)
+    perm1 = one(((pi & 7) == (pj >> 4)) & ((pi >> 3) == (pj & 15)))
+    for j in range(4):
+        sl = slice(j * 256, (j + 1) * 256)
+        sj = s_v[:, sl].astype(bf16)
+        s0[:, :, sl] = dot(sel0, sj).reshape(DS, NB * 2, 256)
+        s1[:, :, sl] = dot(perm1, sj).reshape(DS, REQ, 256)
+
+    lax.fori_loop(1, 2, blocks, 0)
 
     landed(zb, ZB, nt, "tensor")
     proj = jnp.zeros((16, PROJ_PAD), f32)
@@ -353,7 +356,7 @@
     prb[pl.ds(me, 1)] = proj.astype(bf16)[None]
     gather(prb, PR, NB, me, "beam")
 
-    lax.fori_loop(steps // 2, steps, blocks, 0)
+    lax.fori_loop(2, steps, blocks, 0)
     c_suf.wait()
     c_nkv.wait()
     nk0 = nkv_ref[0].astype(f32)
@@ -405,6 +408,19 @@
     gate0 = silu(gate_ref[0].astype(f32))
     gate1 = silu(gate_ref[1].astype(f32))
 
+    held_here = column128(onef(g == me))
+    g1 = one((column128(p1) == (pj >> 3).astype(f32)) & ((pi & 7) == (pj & 7)))
+    r32 = one((iota((32, NB), 0) >> 1) == iota((32, NB), 1))
+    c32 = one((iota((REQ, 128), 1) & 7) == iota((REQ, 128), 0))
+    key32 = dot(dot(r32, key0.astype(bf16)).astype(bf16), c32)
+    si, sj_ = iota((32, 128), 0), iota((32, 128), 1)
+    psl = one((key32 == (si & 1).astype(f32)) & ((si >> 1) == (sj_ >> 3)))
+    ui, uj = iota((256, 256), 0), iota((256, 256), 1)
+    relay = one(((ui >> 4) == ((uj >> 1) & 15)) & (((ui >> 1) & 7) == (uj >> 5)) & ((ui & 1) == (uj & 1)))
+    _, own1 = own_column(p1, me)
+    gi, gj = iota((REQ, 128), 0), iota((REQ, 128), 1)
+    og = one((own1 == (gj >> 3).astype(f32)) & (gi == (gj & 7)))
+
     landed(prb, PR)
     prf = prb[...].astype(f32)
     pr0 = prf[:, 0:REQ, :].reshape(128, PROJ_PAD)
@@ -412,15 +428,9 @@
     rn0 = normed(pr0[:, 0:DT_RANK])
     rn1 = normed(pr1[:, 0:DT_RANK])
     bc0 = pr0[:, DT_RANK:PROJ].astype(bf16)
-    c1[...] = (pr1[:, DT_RANK:PROJ_PAD] * column128(onef(g == me))).reshape(NB, REQ, 128)
-    g1 = one((column128(p1) == (pj >> 3).astype(f32)) & ((pi & 7) == (pj & 7)))
+    c1[...] = (pr1[:, DT_RANK:PROJ_PAD] * held_here).reshape(NB, REQ, 128)
     rn0g = dot(g1, rn0).astype(bf16)
 
-    r32 = one((iota((32, NB), 0) >> 1) == iota((32, NB), 1))
-    c32 = one((iota((REQ, 128), 1) & 7) == iota((REQ, 128), 0))
-    key32 = dot(dot(r32, key0.astype(bf16)).astype(bf16), c32)
-    si, sj_ = iota((32, 128), 0), iota((32, 128), 1)
-    psl = one((key32 == (si & 1).astype(f32)) & ((si >> 1) == (sj_ >> 3)))
     rn0s = dot(psl, rn0).astype(bf16)
     c0s = dot(psl, bc0)
     c0b = [jnp.broadcast_to(c0s[:, DS + n : DS + n + 1], (NB * 2, 128)) for n in range(DS)]
@@ -439,8 +449,6 @@
             acc = acc + cn * (jnp.exp2(dj * (rates_ref[n : n + 1, sl] * (-LOG2E))) * s0[n, :, sl])
         z0 += [acc[:, 0:128], acc[:, 128:256]]
     z0 = jnp.concatenate(z0, axis=0).astype(bf16)
-    ui, uj = iota((256, 256), 0), iota((256, 256), 1)
-    relay = one(((ui >> 4) == ((uj >> 1) & 15)) & (((ui >> 1) & 7) == (uj >> 5)) & ((ui & 1) == (uj & 1)))
     zzs[:, 64:80, :] = dot(relay, z0).astype(bf16).reshape(NB, 16, 128)
 
     def children(i, c):
@@ -465,9 +473,6 @@
     lax.fori_loop(0, NB // 2, children, 0)
     zzr[pl.ds(me, 1)] = zzs[pl.ds(me, 1)]
 
-    _, own1 = own_column(p1, me)
-    gi, gj = iota((REQ, 128), 0), iota((REQ, 128), 1)
-    og = one((own1 == (gj >> 3).astype(f32)) & (gi == (gj & 7)))
     in0p = dot(og, bc0)[:, 0:DS]
     cross = in0p * own_out[REQ : 2 * REQ]
     mixed = jnp.zeros((REQ, CH), f32)
@@ -528,6 +533,15 @@
     sent(zzs, ZZ)
     out_a.wait()
     out_m.wait()
+
+
+def publish(m_ref, a_ref, mo_ref, ao_ref, sem):
+    first = pltpu.make_async_copy(m_ref, mo_ref, sem.at[0])
+    second = pltpu.make_async_copy(a_ref, ao_ref, sem.at[1])
+    first.start()
+    second.start()
+    first.wait()
+    second.wait()
 
 
 def local(
@@ -582,7 +596,7 @@
         jax.ShapeDtypeStruct((2, 1, REQ, CH), bf16),
         jax.ShapeDtypeStruct((2, 1, REQ, GROUP * HD), bf16),
     )
-    return pl.pallas_call(
+    results = pl.pallas_call(
         kernel,
         out_shape=outs,
         in_specs=[hb] * len(operands),
@@ -627,6 +641,15 @@
         ),
         name="decode",
     )(*operands)
+    return pl.pallas_call(
+        publish,
+        out_shape=outs,
+        in_specs=[hb, hb],
+        out_specs=(hb, hb),
+        scratch_shapes=[dma((2,))],
+        compiler_params=pltpu.CompilerParams(vmem_limit_bytes=63 * 2**20),
+        name="publish",
+    )(*results)
 
 
 def solution(mesh):

time: 45.6 us -> 45.8 us (level)
  Pallas kernels: 41.5 us -> 44.5 us
  local copies, waits for them, and re-layouts: 2.7 us -> 0 us
    unnamed x2 -> x0, local copies, waits for them, and re-layouts: 2.7 us -> none
    pallas_call x0 -> x1, Pallas kernels: none -> 2.61 us  [local(): pl.pallas_call(publish, out_shape=outs, in_specs=[hb, hb], out_specs=(hb,...]
where the time goes in v2:
time: 45.8 us; the launch traced here: 45.1 us
  Pallas kernels  44.5 us (97%)
  between operations  0.65 us (1%)
    pallas_call x1, Pallas kernels, local(): pl.pallas_call(kernel, out_shape=outs, in_specs=[hb] * len(operands), out...  41.8 us
    pallas_call x1, Pallas kernels, local(): pl.pallas_call(publish, out_shape=outs, in_specs=[hb, hb], out_specs=(hb,...  2.61 us

profile of v2, /device:TPU:2, one launch (start us, length us, event | category | flops | bytes accessed | tf_op | source)
XLA Modules:
  0.0 45.1 jit_solution(15608519813846374746)
XLA Ops:
  0.6 41.8 %decode.1 = (bf16[2,1,8,1024]{3,2,1,0:T(8,128)(2,1)}, bf16[2,1,8,512]{3,2,1,0:T(8,128)(2,1)}) custom-call(s32[16,16]{1,0:T(8,128)} %bitcast.26, s32[32,128]{1,0:T(8,128)} %bitcast.24, s32[8]{0:T(128)} %ctx_h.1, bf16[3,8,1024]{2,1,0:T(8,128)(2,1)} %bitcast.21, bf16[4,1024]{1,0:T(4,128)(2,1)} %cw_h.1, bf16[8,128]{1,0:T(8,128)(2,1)} %bitcast.30, ...), custom_call_target="tpu_custom_call" | custom-call | tf_op jit(solution)/shard_map/decode/pallas_call | solution.py:599
  42.5 2.6 %publish.1 = (bf16[2,1,8,1024]{3,2,1,0:T(8,128)(2,1)}, bf16[2,1,8,512]{3,2,1,0:T(8,128)(2,1)}) custom-call(bf16[2,1,8,1024]{3,2,1,0:T(8,128)(2,1)} %get-tuple-element.4.m_ref, bf16[2,1,8,512]{3,2,1,0:T(8,128)(2,1)} %get-tuple-element.5.a_ref), custom_call_target="tpu_custom_call" | custom-call | tf_op jit(solution)/shard_map/publish/pallas_call | solution.py:644

commit v3 on v2

--- a/solution.py
+++ b/solution.py
@@ -114,14 +114,14 @@
     par_ref, po_ref, ctx_ref, cs_ref, cw_ref, cb_ref, x_ref, gate_ref, q_ref, nkv_ref, suf_ref, gain_ref, dtb_ref,
     rates_ref, skip_ref, s_v, xw_v, dtw_v, kv_v,
     mo_ref, ao_ref,
-    h1s, h1r, h2s, h2r, qa, zb, prb, zzs, zzr, os_, or_, lse,
+    h1s, h1r, has, har, h2s, h2r, hcs, hcr, qa, zb, prb, zzs, zzr, os_, or_, lse,
     tab, tabs, bias, qr, orun, mrun, osf, s0, s1, rt, d1, d0g, c1, okm,
     lsem, tsem, ssem, rsem,
 ):
     me = lax.axis_index("beam")
     mt = lax.axis_index("tensor")
     nt = zb.shape[0]
-    H1, H2, QA, ZB, PR, OO, LS, ZZ = range(8)
+    H1, H2, QA, ZB, PR, OO, LS, ZZ, HA, HC = range(10)
 
     def push(src, dst, to, k, axis):
         pltpu.make_async_remote_copy(
@@ -183,8 +183,10 @@
     a1 = win[1] * cw_row[0] + win[2] * cw_row[1]
     both = jnp.concatenate([to_rows(a0), to_rows(a1)], axis=1).astype(bf16)
     packed = dot(pack_matrix(key0), both).astype(bf16)
-    h1s[...] = packed.reshape(NB, 16, 256)
+    h1s[...] = packed[:, 128:256].reshape(NB, 16, 128)
+    has[...] = packed[:, 0:128].reshape(NB, 16, 128)
     h1r[pl.ds(me, 1)] = h1s[pl.ds(me, 1)]
+    har[pl.ds(me, 1)] = has[pl.ds(me, 1)]
 
     c_q.wait()
     qrows = jnp.concatenate(
@@ -197,7 +199,7 @@
     pl.semaphore_wait(barrier, NB - 1 + nt - 1)
 
     exchange(h1s, h1r, H1)
-    gather(qa, QA, NB, me, "beam")
+    exchange(has, har, HA)
 
     key1 = slot_key(p1, me)
     pb1 = pack_matrix(key1)
@@ -206,6 +208,26 @@
     g = jnp.zeros((NB, REQ), i32)
     for p in range(NB):
         g = g + jnp.where(p1 == p, p0[p : p + 1, :], 0)
+    c_x.wait()
+    c_cb.wait()
+    x0 = x_ref[0].astype(f32)
+    x1 = x_ref[1].astype(f32)
+    cb8 = cb_ref[...].astype(f32)
+    cb = jnp.concatenate([cb8[i : i + 1] for i in range(LT)], axis=1)
+
+    landed(h1r, H1)
+    w1 = from_rows(dot(ub0, h1r[...].reshape(NB * 16, 128))) + cw_row[2] * x0
+    h2s[...] = dot(pb1, to_rows(w1).astype(bf16)).astype(bf16).reshape(NB, 16, 128)
+    h2r[pl.ds(me, 1)] = h2s[pl.ds(me, 1)]
+    exchange(h2s, h2r, H2)
+    gather(qa, QA, NB, me, "beam")
+
+    landed(har, HA)
+    c0 = from_rows(dot(ub0, har[...].reshape(NB * 16, 128))) + cw_row[3] * x0 + cb
+    conv0 = silu(c0)
+    hcs[...] = dot(pb1, to_rows(conv0).astype(bf16)).astype(bf16).reshape(NB, 16, 128)
+    hcr[pl.ds(me, 1)] = hcs[pl.ds(me, 1)]
+
     c_po.wait()
     c_ctx.wait()
     ctx_col = jnp.zeros((REQ, MAXP), i32)
@@ -261,21 +283,45 @@
     mrun[0] = jnp.full((128, HD), NEG, f32)
     cp_tab.wait()
 
-    c_x.wait()
-    c_cb.wait()
-    x0 = x_ref[0].astype(f32)
-    x1 = x_ref[1].astype(f32)
-    cb8 = cb_ref[...].astype(f32)
-    cb = jnp.concatenate([cb8[i : i + 1] for i in range(LT)], axis=1)
-
-    landed(h1r, H1)
-    got = dot(ub0, h1r[...].reshape(NB * 16, 256))
-    c0 = from_rows(got[:, 0:128]) + cw_row[3] * x0 + cb
-    w1 = from_rows(got[:, 128:256]) + cw_row[2] * x0
-    both = jnp.concatenate([to_rows(c0), to_rows(w1)], axis=1).astype(bf16)
-    h2s[...] = dot(pb1, both).astype(bf16).reshape(NB, 16, 256)
-    h2r[pl.ds(me, 1)] = h2s[pl.ds(me, 1)]
-    exchange(h2s, h2r, H2)
+    c_xw.wait()
+    landed(h2r, H2)
+    conv1 = silu(from_rows(dot(ub1, h2r[...].reshape(NB * 16, 128))) + cw_row[3] * x1 + cb)
+    part = dot_nt(jnp.concatenate([conv0, conv1], axis=0).astype(bf16), xw_v[...])
+    zb[pl.ds(mt, 1)] = jnp.zeros((1, 16, PROJ_PAD), bf16)
+    zb[pl.ds(mt, 1), :, 0:PROJ] = part.astype(bf16)[None]
+    gather(zb, ZB, nt, mt, "tensor")
+    exchange(hcs, hcr, HC)
+
+
+    wide = one((iota((REQ, REQ * 128), 1) >> 7) == iota((REQ, REQ * 128), 0))
+    x_s0 = dot(one(p0 == me), wide)
+    x_sg = dot(one(g == me), wide)
+    x_s1 = dot(one(p1 == me), wide)
+    tok = iota((NB, REQ * 128), 1) & 127
+    mine = onef(iota((NB, REQ * 128), 0) == me)
+    ok0 = jnp.where(tok < 16, x_s0, jnp.where(tok == 16, mine, 0.0))
+    ok1 = jnp.where(tok < 16, x_sg, jnp.where(tok == 16, x_s1, jnp.where(tok == 17, mine, 0.0)))
+    qi, qj = iota((128, 2 * NB), 0), iota((128, 2 * NB), 1)
+    pick = one((((qi >> 2) & 1) == (qj >> 4)) & ((qi >> 3) == (qj & 15)))
+    okm[...] = dot(pick, jnp.concatenate([ok0, ok1], axis=0).astype(bf16))
+
+    c_rates.wait()
+    for n in range(DS):
+        rt[n] = jnp.broadcast_to(rates_ref[n : n + 1, :] * (-LOG2E), (REQ, CH))
+    c_s.wait()
+    row, col = iota((DS * NB * 2, 128), 0), iota((DS * NB * 2, 128), 1)
+    rs_ = one(((iota((DS * NB * 2, NB), 0) >> 1) & 15) == iota((DS * NB * 2, NB), 1))
+    crn = one((iota((REQ, 128), 1) >> 4) == iota((REQ, 128), 0))
+    keys = dot(rs_, dot(key0.astype(bf16), crn).astype(bf16))
+    sel0 = one((keys == (row & 1).astype(f32)) & ((row >> 5) == (col & 15)))
+    pi, pj = iota((128, 128), 0), iota((128, 128), 1)
+    perm1 = one(((pi & 7) == (pj >> 4)) & ((pi >> 3) == (pj & 15)))
+    for j in range(4):
+        sl = slice(j * 256, (j + 1) * 256)
+        sj = s_v[:, sl].astype(bf16)
+        s0[:, :, sl] = dot(sel0, sj).reshape(DS, NB * 2, 256)
+        s1[:, :, sl] = dot(perm1, sj).reshape(DS, REQ, 256)
+
 
     landed(qa, QA)
     qf = qa[...].astype(f32)
@@ -304,50 +350,7 @@
         return c
 
     steps = NBLK // UNROLL
-    lax.fori_loop(0, 1, blocks, 0)
-
-    c_xw.wait()
-    landed(h2r, H2)
-    got = dot(ub1, h2r[...].reshape(NB * 16, 256))
-    conv0p = silu(from_rows(got[:, 0:128]))
-    conv0 = silu(c0)
-    conv1 = silu(from_rows(got[:, 128:256]) + cw_row[3] * x1 + cb)
-    part = dot_nt(jnp.concatenate([conv0, conv1], axis=0).astype(bf16), xw_v[...])
-    zb[pl.ds(mt, 1)] = jnp.zeros((1, 16, PROJ_PAD), bf16)
-    zb[pl.ds(mt, 1), :, 0:PROJ] = part.astype(bf16)[None]
-    gather(zb, ZB, nt, mt, "tensor")
-
-
-    wide = one((iota((REQ, REQ * 128), 1) >> 7) == iota((REQ, REQ * 128), 0))
-    x_s0 = dot(one(p0 == me), wide)
-    x_sg = dot(one(g == me), wide)
-    x_s1 = dot(one(p1 == me), wide)
-    tok = iota((NB, REQ * 128), 1) & 127
-    mine = onef(iota((NB, REQ * 128), 0) == me)
-    ok0 = jnp.where(tok < 16, x_s0, jnp.where(tok == 16, mine, 0.0))
-    ok1 = jnp.where(tok < 16, x_sg, jnp.where(tok == 16, x_s1, jnp.where(tok == 17, mine, 0.0)))
-    qi, qj = iota((128, 2 * NB), 0), iota((128, 2 * NB), 1)
-    pick = one((((qi >> 2) & 1) == (qj >> 4)) & ((qi >> 3) == (qj & 15)))
-    okm[...] = dot(pick, jnp.concatenate([ok0, ok1], axis=0).astype(bf16))
-
-    c_rates.wait()
-    for n in range(DS):
-        rt[n] = jnp.broadcast_to(rates_ref[n : n + 1, :] * (-LOG2E), (REQ, CH))
-    c_s.wait()
-    row, col = iota((DS * NB * 2, 128), 0), iota((DS * NB * 2, 128), 1)
-    rs_ = one(((iota((DS * NB * 2, NB), 0) >> 1) & 15) == iota((DS * NB * 2, NB), 1))
-    crn = one((iota((REQ, 128), 1) >> 4) == iota((REQ, 128), 0))
-    keys = dot(rs_, dot(key0.astype(bf16), crn).astype(bf16))
-    sel0 = one((keys == (row & 1).astype(f32)) & ((row >> 5) == (col & 15)))
-    pi, pj = iota((128, 128), 0), iota((128, 128), 1)
-    perm1 = one(((pi & 7) == (pj >> 4)) & ((pi >> 3) == (pj & 15)))
-    for j in range(4):
-        sl = slice(j * 256, (j + 1) * 256)
-        sj = s_v[:, sl].astype(bf16)
-        s0[:, :, sl] = dot(sel0, sj).reshape(DS, NB * 2, 256)
-        s1[:, :, sl] = dot(perm1, sj).reshape(DS, REQ, 256)
-
-    lax.fori_loop(1, 2, blocks, 0)
+    lax.fori_loop(0, 2, blocks, 0)
 
     landed(zb, ZB, nt, "tensor")
     proj = jnp.zeros((16, PROJ_PAD), f32)
@@ -473,6 +476,8 @@
     lax.fori_loop(0, NB // 2, children, 0)
     zzr[pl.ds(me, 1)] = zzs[pl.ds(me, 1)]
 
+    landed(hcr, HC)
+    conv0p = from_rows(dot(ub1, hcr[...].reshape(NB * 16, 128)))
     in0p = dot(og, bc0)[:, 0:DS]
     cross = in0p * own_out[REQ : 2 * REQ]
     mixed = jnp.zeros((REQ, CH), f32)
@@ -524,7 +529,9 @@
     out_m.start()
 
     sent(h1s, H1)
+    sent(has, HA)
     sent(h2s, H2)
+    sent(hcs, HC)
     sent(qa, QA)
     sent(zb, ZB, nt, "tensor")
     sent(prb, PR)
@@ -535,10 +542,16 @@
     out_m.wait()
 
 
-def publish(m_ref, a_ref, mo_ref, ao_ref, sem):
-    first = pltpu.make_async_copy(m_ref, mo_ref, sem.at[0])
-    second = pltpu.make_async_copy(a_ref, ao_ref, sem.at[1])
+def publish(m_ref, a_ref, mo_ref, ao_ref, m_v, a_v, sem):
+    first = pltpu.make_async_copy(m_ref, m_v, sem.at[0])
+    second = pltpu.make_async_copy(a_ref, a_v, sem.at[1])
     first.start()
+    second.start()
+    first.wait()
+    first = pltpu.make_async_copy(m_v, mo_ref, sem.at[0])
+    first.start()
+    second.wait()
+    second = pltpu.make_async_copy(a_v, ao_ref, sem.at[1])
     second.start()
     first.wait()
     second.wait()
@@ -605,10 +618,14 @@
         + [
             V(outs[0].shape, bf16),
             V(outs[1].shape, bf16),
-            V((NB, 16, 256), bf16),
-            V((NB, 16, 256), bf16),
-            V((NB, 16, 256), bf16),
-            V((NB, 16, 256), bf16),
+            V((NB, 16, 128), bf16),
+            V((NB, 16, 128), bf16),
+            V((NB, 16, 128), bf16),
+            V((NB, 16, 128), bf16),
+            V((NB, 16, 128), bf16),
+            V((NB, 16, 128), bf16),
+            V((NB, 16, 128), bf16),
+            V((NB, 16, 128), bf16),
             V((NB, 64, HD), bf16),
             V((nt, 16, PROJ_PAD), bf16),
             V((NB, 16, PROJ_PAD), bf16),
@@ -633,8 +650,8 @@
             V((128, REQ * 128), f32),
             dma((len(operands),)),
             dma,
-            dma((8,)),
-            dma((8,)),
+            dma((10,)),
+            dma((10,)),
         ],
         compiler_params=pltpu.CompilerParams(
             collective_id=0, has_side_effects=True, vmem_limit_bytes=63 * 2**20
@@ -646,7 +663,7 @@
         out_shape=outs,
         in_specs=[hb, hb],
         out_specs=(hb, hb),
-        scratch_shapes=[dma((2,))],
+        scratch_shapes=[V(outs[0].shape, bf16), V(outs[1].shape, bf16), dma((2,))],
         compiler_params=pltpu.CompilerParams(vmem_limit_bytes=63 * 2**20),
         name="publish",
     )(*results)

time: 45.8 us -> 43.1 us (0.941)
  Pallas kernels: 44.5 us -> 41.7 us
    pallas_call x1, Pallas kernels: 41.8 us -> 40.4 us  [local(): pl.pallas_call(kernel, out_shape=outs, in_specs=[hb] * len(operands), out...]
    pallas_call x1, Pallas kernels: 2.61 us -> 1.39 us  [local(): pl.pallas_call(publish, out_shape=outs, in_specs=[hb, hb], out_specs=(hb,...]
where the time goes in v3:
time: 43.1 us; the launch traced here: 42.4 us
  Pallas kernels  41.7 us (97%)
  between operations  0.65 us (2%)
    pallas_call x1, Pallas kernels, local(): pl.pallas_call(kernel, out_shape=outs, in_specs=[hb] * len(operands), out...  40.4 us
    pallas_call x1, Pallas kernels, local(): pl.pallas_call(publish, out_shape=outs, in_specs=[hb, hb], out_specs=(hb,...  1.39 us

profile of v3, /device:TPU:2, one launch (start us, length us, event | category | flops | bytes accessed | tf_op | source)
XLA Modules:
  0.0 42.4 jit_solution(564829940685142077)
XLA Ops:
  0.6 40.4 %decode.1 = (bf16[2,1,8,1024]{3,2,1,0:T(8,128)(2,1)}, bf16[2,1,8,512]{3,2,1,0:T(8,128)(2,1)}) custom-call(s32[16,16]{1,0:T(8,128)} %bitcast.26, s32[32,128]{1,0:T(8,128)} %bitcast.24, s32[8]{0:T(128)} %ctx_h.1, bf16[3,8,1024]{2,1,0:T(8,128)(2,1)} %bitcast.21, bf16[4,1024]{1,0:T(4,128)(2,1)} %cw_h.1, bf16[8,128]{1,0:T(8,128)(2,1)} %bitcast.30, ...), custom_call_target="tpu_custom_call" | custom-call | tf_op jit(solution)/shard_map/decode/pallas_call | solution.py:612
  41.0 1.4 %publish.1 = (bf16[2,1,8,1024]{3,2,1,0:T(8,128)(2,1)}, bf16[2,1,8,512]{3,2,1,0:T(8,128)(2,1)}) custom-call(bf16[2,1,8,1024]{3,2,1,0:T(8,128)(2,1)} %get-tuple-element.4.m_ref, bf16[2,1,8,512]{3,2,1,0:T(8,128)(2,1)} %get-tuple-element.5.a_ref), custom_call_target="tpu_custom_call" | custom-call | tf_op jit(solution)/shard_map/publish/pallas_call | solution.py:661

commit v4 on v3

--- a/solution.py
+++ b/solution.py
@@ -114,42 +114,50 @@
     par_ref, po_ref, ctx_ref, cs_ref, cw_ref, cb_ref, x_ref, gate_ref, q_ref, nkv_ref, suf_ref, gain_ref, dtb_ref,
     rates_ref, skip_ref, s_v, xw_v, dtw_v, kv_v,
     mo_ref, ao_ref,
-    h1s, h1r, has, har, h2s, h2r, hcs, hcr, qa, zb, prb, zzs, zzr, os_, or_, lse,
+    h1s, h1r, has, har, h2s, h2r, hcs, hcr, qa, pv, pas, par_r, zb, both_pr, zzs, zzr, os_, or_, lse,
     tab, tabs, bias, qr, orun, mrun, osf, s0, s1, rt, d1, d0g, c1, okm,
     lsem, tsem, ssem, rsem,
 ):
     me = lax.axis_index("beam")
     mt = lax.axis_index("tensor")
-    nt = zb.shape[0]
-    H1, H2, QA, ZB, PR, OO, LS, ZZ, HA, HC = range(10)
-
-    def push(src, dst, to, k, axis):
-        pltpu.make_async_remote_copy(
-            src_ref=src, dst_ref=dst, send_sem=ssem.at[k], recv_sem=rsem.at[k], device_id={axis: to},
+    nz = zb.shape[0]
+    core, mz = mt & 1, mt >> 1
+    other = mt + 1 - 2 * core
+    H1, H2, QA, ZB, PR, OO, LS, ZZ, HA, HC, PA, SW = range(12)
+
+    def beam_peer(d):
+        return ((me + d) & (NB - 1), mt)
+
+    def z_peer(d):
+        return (me, (((mz + d) & (nz - 1)) << 1) + core)
+
+    def remote(src, dst, k, device):
+        return pltpu.make_async_remote_copy(
+            src_ref=src, dst_ref=dst, send_sem=ssem.at[k], recv_sem=rsem.at[k], device_id=device,
             device_id_type=MESH,
-        ).start()
+        )
 
     def exchange(src, dst, k):
         for d in range(1, NB):
-            peer = lax.rem(me + d, NB)
-            push(src.at[peer], dst.at[me], peer, k, "beam")
-
-    def gather(buf, k, n, my, axis):
-        for d in range(1, n):
-            push(buf.at[my], buf.at[my], lax.rem(my + d, n), k, axis)
-
-    def all_of(buf, k, n, axis):
-        part = buf.at[pl.ds(0, n - 1)]
-        return pltpu.make_async_remote_copy(
-            src_ref=part, dst_ref=part, send_sem=ssem.at[k], recv_sem=rsem.at[k], device_id={axis: 0},
-            device_id_type=MESH,
-        )
-
-    def landed(buf, k, n=NB, axis="beam"):
-        all_of(buf, k, n, axis).wait_recv()
-
-    def sent(buf, k, n=NB, axis="beam"):
-        all_of(buf, k, n, axis).wait_send()
+            peer = beam_peer(d)
+            remote(src.at[peer[0]], dst.at[me], k, peer).start()
+
+    def gather(buf, k, at, peers):
+        for peer in peers:
+            remote(buf.at[at], buf.at[at], k, peer).start()
+
+    beam_peers = [beam_peer(d) for d in range(1, NB)]
+    z_peers = [z_peer(d) for d in range(1, nz)]
+
+    def all_of(buf, k):
+        part = buf.at[pl.ds(0, buf.shape[0] - 1)]
+        return remote(part, part, k, (me, mt))
+
+    def landed(buf, k):
+        all_of(buf, k).wait_recv()
+
+    def sent(buf, k):
+        all_of(buf, k).wait_send()
 
     pairs = [
         (par_h, par_ref), (cs_h, cs_ref), (cw_h, cw_ref), (q_h, q_ref), (s_h, s_v), (rates_h, rates_ref),
@@ -160,13 +168,14 @@
     copies = [pltpu.make_async_copy(a, b, lsem.at[i]) for i, (a, b) in enumerate(pairs)]
     (c_par, c_cs, c_cw, c_q, c_s, c_rates, c_x, c_cb, c_po, c_ctx, c_xw, c_kv, c_suf, c_nkv, c_dtw, c_dtb, c_gain,
      c_skip, c_gate) = copies
-    for c in copies:
+    for c in copies[0:4]:
         c.start()
     barrier = pltpu.get_barrier_semaphore()
-    for d in range(1, NB):
-        pl.semaphore_signal(barrier, inc=1, device_id={"beam": lax.rem(me + d, NB)}, device_id_type=MESH)
-    for d in range(1, nt):
-        pl.semaphore_signal(barrier, inc=1, device_id={"tensor": lax.rem(mt + d, nt)}, device_id_type=MESH)
+    greeted = beam_peers + z_peers + [(me, other)]
+    for peer in greeted:
+        pl.semaphore_signal(barrier, inc=1, device_id=peer, device_id_type=MESH)
+    for c in copies[4:]:
+        c.start()
 
     c_par.wait()
     par_t = par_ref[...].astype(f32).astype(bf16)
@@ -196,7 +205,7 @@
     swap = one(((ri >> 3) == (ci & 7)) & ((ri & 7) == (ci >> 3)))
     qa[pl.ds(me, 1)] = dot(swap, qrows).astype(bf16)[None]
 
-    pl.semaphore_wait(barrier, NB - 1 + nt - 1)
+    pl.semaphore_wait(barrier, len(greeted))
 
     exchange(h1s, h1r, H1)
     exchange(has, har, HA)
@@ -220,7 +229,7 @@
     h2s[...] = dot(pb1, to_rows(w1).astype(bf16)).astype(bf16).reshape(NB, 16, 128)
     h2r[pl.ds(me, 1)] = h2s[pl.ds(me, 1)]
     exchange(h2s, h2r, H2)
-    gather(qa, QA, NB, me, "beam")
+    gather(qa, QA, me, beam_peers)
 
     landed(har, HA)
     c0 = from_rows(dot(ub0, har[...].reshape(NB * 16, 128))) + cw_row[3] * x0 + cb
@@ -283,14 +292,27 @@
     mrun[0] = jnp.full((128, HD), NEG, f32)
     cp_tab.wait()
 
+    pv[...] = jnp.zeros_like(pv)
+
     c_xw.wait()
     landed(h2r, H2)
     conv1 = silu(from_rows(dot(ub1, h2r[...].reshape(NB * 16, 128))) + cw_row[3] * x1 + cb)
     part = dot_nt(jnp.concatenate([conv0, conv1], axis=0).astype(bf16), xw_v[...])
-    zb[pl.ds(mt, 1)] = jnp.zeros((1, 16, PROJ_PAD), bf16)
-    zb[pl.ds(mt, 1), :, 0:PROJ] = part.astype(bf16)[None]
-    gather(zb, ZB, nt, mt, "tensor")
+    pv[:, 0:PROJ] = part
+
+    def packed8(at):
+        x = pv[pl.ds(pl.multiple_of(at * REQ, REQ), REQ), :]
+        rank_rows = jnp.concatenate([x[:, 0:128], x[:, 128:256]], axis=0)
+        maps = jnp.concatenate([x[:, 256:384], jnp.zeros((REQ, 128), f32)], axis=0)
+        return jnp.concatenate([rank_rows, maps], axis=1)
+
+    pas[...] = packed8(1 - core)
+    to_core = remote(pas, par_r, PA, (me, other))
+    to_core.start()
     exchange(hcs, hcr, HC)
+    to_core.wait_recv()
+    zb[pl.ds(mz, 1)] = (packed8(core) + par_r[...]).astype(bf16)[None]
+    gather(zb, ZB, mz, z_peers)
 
 
     wide = one((iota((REQ, REQ * 128), 1) >> 7) == iota((REQ, REQ * 128), 0))
@@ -352,12 +374,13 @@
     steps = NBLK // UNROLL
     lax.fori_loop(0, 2, blocks, 0)
 
-    landed(zb, ZB, nt, "tensor")
-    proj = jnp.zeros((16, PROJ_PAD), f32)
-    for t in range(nt):
+    landed(zb, ZB)
+    proj = jnp.zeros((16, 256), f32)
+    for t in range(nz):
         proj = proj + zb[t].astype(f32)
-    prb[pl.ds(me, 1)] = proj.astype(bf16)[None]
-    gather(prb, PR, NB, me, "beam")
+    mine_pr = both_pr.at[core]
+    mine_pr[pl.ds(me, 1)] = proj.astype(bf16)[None]
+    gather(mine_pr, PR, me, beam_peers)
 
     lax.fori_loop(2, steps, blocks, 0)
     c_suf.wait()
@@ -388,7 +411,7 @@
     os_[...] = osf[...].astype(bf16)
     or_[pl.ds(me, 1)] = os_[pl.ds(me, 1)]
     exchange(os_, or_, OO)
-    gather(lse, LS, NB, me, "beam")
+    gather(lse, LS, me, beam_peers)
 
     for c in (c_dtw, c_dtb, c_gain, c_skip, c_gate):
         c.wait()
@@ -399,15 +422,6 @@
         return (rank_rows * lax.rsqrt(mean + 1e-6) * gain).astype(bf16)
 
     dtb = dtb_ref[...]
-    own = proj.astype(bf16).astype(f32)
-    d_own = softplus(dot(normed(own[:, 0:DT_RANK]), dtw_v[...]) + dtb)
-    d_own0, d_own1 = d_own[0:REQ], d_own[REQ : 2 * REQ]
-    own_in = own[:, DT_RANK : DT_RANK + DS]
-    own_out = own[:, DT_RANK + DS : DT_RANK + 2 * DS]
-    cb_own = jnp.sum(own_in * own_out, axis=1, keepdims=True)
-    skip = skip_ref[...]
-    base0 = d_own0 * conv0 * cb_own[0:REQ] + skip * conv0
-    base1 = d_own1 * conv1 * cb_own[REQ : 2 * REQ] + skip * conv1
     gate0 = silu(gate_ref[0].astype(f32))
     gate1 = silu(gate_ref[1].astype(f32))
 
@@ -424,14 +438,21 @@
     gi, gj = iota((REQ, 128), 0), iota((REQ, 128), 1)
     og = one((own1 == (gj >> 3).astype(f32)) & (gi == (gj & 7)))
 
-    landed(prb, PR)
-    prf = prb[...].astype(f32)
-    pr0 = prf[:, 0:REQ, :].reshape(128, PROJ_PAD)
-    pr1 = prf[:, REQ : 2 * REQ, :].reshape(128, PROJ_PAD)
-    rn0 = normed(pr0[:, 0:DT_RANK])
-    rn1 = normed(pr1[:, 0:DT_RANK])
-    bc0 = pr0[:, DT_RANK:PROJ].astype(bf16)
-    c1[...] = (pr1[:, DT_RANK:PROJ_PAD] * held_here).reshape(NB, REQ, 128)
+    landed(mine_pr, PR)
+    swap_cores = remote(mine_pr, mine_pr, SW, (me, other))
+    swap_cores.start()
+    swap_cores.wait_recv()
+
+    def unpacked(x):
+        x = x.astype(f32)
+        return jnp.concatenate([x[..., 0:REQ, 0:128], x[..., REQ : 2 * REQ, 0:128]], axis=-1), x[..., 0:REQ, 128:256]
+
+    rank0, maps0 = unpacked(both_pr[0])
+    rank1, maps1 = unpacked(both_pr[1])
+    rn0 = normed(rank0.reshape(128, DT_RANK))
+    rn1 = normed(rank1.reshape(128, DT_RANK))
+    bc0 = maps0.reshape(128, 128)[:, 0 : 2 * DS].astype(bf16)
+    c1[...] = (maps1.reshape(128, 128) * held_here).reshape(NB, REQ, 128)
     rn0g = dot(g1, rn0).astype(bf16)
 
     rn0s = dot(psl, rn0).astype(bf16)
@@ -455,7 +476,7 @@
     zzs[:, 64:80, :] = dot(relay, z0).astype(bf16).reshape(NB, 16, 128)
 
     def children(i, c):
-        two = [lax.rem(me + 1 + 2 * i, NB), lax.rem(me + 2 + 2 * i, NB)]
+        two = [(me + 1 + 2 * i) & (NB - 1), (me + 2 + 2 * i) & (NB - 1)]
         outs = [c1[b] for b in two]
         deltas = [d1[b] for b in two]
         accs = [jnp.zeros((REQ, CH), f32) for _ in two]
@@ -465,21 +486,31 @@
                 accs[k] = accs[k] + outs[k][:, DS + n : DS + n + 1] * (jnp.exp2(deltas[k] * rn) * sn)
         for k in range(2):
             zzs[two[k], 0:64, :] = to_rows(accs[k]).astype(bf16)
-        push(zzs.at[two[0]], zzr.at[me], two[0], ZZ, "beam")
+        remote(zzs.at[two[0]], zzr.at[me], ZZ, (two[0], mt)).start()
 
         @pl.when(i < NB // 2 - 1)
         def _():
-            push(zzs.at[two[1]], zzr.at[me], two[1], ZZ, "beam")
+            remote(zzs.at[two[1]], zzr.at[me], ZZ, (two[1], mt)).start()
 
         return c
 
     lax.fori_loop(0, NB // 2, children, 0)
     zzr[pl.ds(me, 1)] = zzs[pl.ds(me, 1)]
+
+    own_rank, own_maps = zip(*[unpacked(both_pr[s, pl.ds(me, 1)][0]) for s in range(2)])
+    d_own = softplus(dot(normed(jnp.concatenate(own_rank, axis=0)), dtw_v[...]) + dtb)
+    d_own0, d_own1 = d_own[0:REQ], d_own[REQ : 2 * REQ]
+    own_in = [m[:, 0:DS] for m in own_maps]
+    own_out = [m[:, DS : 2 * DS] for m in own_maps]
+    cb_own = [jnp.sum(a * b, axis=1, keepdims=True) for a, b in zip(own_in, own_out)]
+    skip = skip_ref[...]
+    base0 = d_own0 * conv0 * cb_own[0] + skip * conv0
+    base1 = d_own1 * conv1 * cb_own[1] + skip * conv1
 
     landed(hcr, HC)
     conv0p = from_rows(dot(ub1, hcr[...].reshape(NB * 16, 128)))
     in0p = dot(og, bc0)[:, 0:DS]
-    cross = in0p * own_out[REQ : 2 * REQ]
+    cross = in0p * own_out[1]
     mixed = jnp.zeros((REQ, CH), f32)
     for n in range(DS):
         mixed = mixed + cross[:, n : n + 1] * jnp.exp2(d_own1 * rt[n])
@@ -533,8 +564,10 @@
     sent(h2s, H2)
     sent(hcs, HC)
     sent(qa, QA)
-    sent(zb, ZB, nt, "tensor")
-    sent(prb, PR)
+    to_core.wait_send()
+    sent(zb, ZB)
+    sent(mine_pr, PR)
+    swap_cores.wait_send()
     sent(os_, OO)
     sent(lse, LS)
     sent(zzs, ZZ)
@@ -627,8 +660,11 @@
             V((NB, 16, 128), bf16),
             V((NB, 16, 128), bf16),
             V((NB, 64, HD), bf16),
-            V((nt, 16, PROJ_PAD), bf16),
-            V((NB, 16, PROJ_PAD), bf16),
+            V((16, PROJ_PAD), f32),
+            V((16, 256), f32),
+            V((16, 256), f32),
+            V((nt // 2, 16, 256), bf16),
+            V((2, NB, 16, 256), bf16),
             V((NB, 80, 128), bf16),
             V((NB, 80, 128), bf16),
             V((NB, 64, HD), bf16),
@@ -650,8 +686,8 @@
             V((128, REQ * 128), f32),
             dma((len(operands),)),
             dma,
-            dma((10,)),
-            dma((10,)),
+            dma((12,)),
+            dma((12,)),
         ],
         compiler_params=pltpu.CompilerParams(
             collective_id=0, has_side_effects=True, vmem_limit_bytes=63 * 2**20

time: 43.1 us -> 44.8 us (1.039)
  the two profiles are of different devices: /device:TPU:2 before, /device:TPU:1 now
where the time goes in v4:
time: 44.8 us; the launch traced here: 44.7 us
  Pallas kernels  44 us (98%)
  between operations  0.65 us (1%)
    pallas_call x1, Pallas kernels, local(): pl.pallas_call(kernel, out_shape=outs, in_specs=[hb] * len(operands), out...  42.6 us
    pallas_call x1, Pallas kernels, local(): pl.pallas_call(publish, out_shape=outs, in_specs=[hb, hb], out_specs=(hb,...  1.39 us

profile of v4, /device:TPU:1, one launch (start us, length us, event | category | flops | bytes accessed | tf_op | source)
XLA Modules:
  0.0 44.7 jit_solution(11678281339185751730)
XLA Ops:
  0.6 42.6 %decode.1 = (bf16[2,1,8,1024]{3,2,1,0:T(8,128)(2,1)}, bf16[2,1,8,512]{3,2,1,0:T(8,128)(2,1)}) custom-call(s32[16,16]{1,0:T(8,128)} %bitcast.26, s32[32,128]{1,0:T(8,128)} %bitcast.24, s32[8]{0:T(128)} %ctx_h.1, bf16[3,8,1024]{2,1,0:T(8,128)(2,1)} %bitcast.21, bf16[4,1024]{1,0:T(4,128)(2,1)} %cw_h.1, bf16[8,128]{1,0:T(8,128)(2,1)} %bitcast.30, ...), custom_call_target="tpu_custom_call" | custom-call | tf_op jit(solution)/shard_map/decode/pallas_call | solution.py:645
  43.3 1.4 %publish.1 = (bf16[2,1,8,1024]{3,2,1,0:T(8,128)(2,1)}, bf16[2,1,8,512]{3,2,1,0:T(8,128)(2,1)}) custom-call(bf16[2,1,8,1024]{3,2,1,0:T(8,128)(2,1)} %get-tuple-element.4.m_ref, bf16[2,1,8,512]{3,2,1,0:T(8,128)(2,1)} %get-tuple-element.5.a_ref), custom_call_target="tpu_custom_call" | custom-call | tf_op jit(solution)/shard_map/publish/pallas_call | solution.py:697

commit v5 on v3

--- a/solution.py
+++ b/solution.py
@@ -114,59 +114,59 @@
     par_ref, po_ref, ctx_ref, cs_ref, cw_ref, cb_ref, x_ref, gate_ref, q_ref, nkv_ref, suf_ref, gain_ref, dtb_ref,
     rates_ref, skip_ref, s_v, xw_v, dtw_v, kv_v,
     mo_ref, ao_ref,
-    h1s, h1r, has, har, h2s, h2r, hcs, hcr, qa, zb, prb, zzs, zzr, os_, or_, lse,
+    h1s, h1r, hcs, hcr, qa, zb, prb, zzs, zzr, os_, or_, lse,
     tab, tabs, bias, qr, orun, mrun, osf, s0, s1, rt, d1, d0g, c1, okm,
     lsem, tsem, ssem, rsem,
 ):
     me = lax.axis_index("beam")
     mt = lax.axis_index("tensor")
     nt = zb.shape[0]
-    H1, H2, QA, ZB, PR, OO, LS, ZZ, HA, HC = range(10)
-
-    def push(src, dst, to, k, axis):
-        pltpu.make_async_remote_copy(
-            src_ref=src, dst_ref=dst, send_sem=ssem.at[k], recv_sem=rsem.at[k], device_id={axis: to},
-            device_id_type=MESH,
-        ).start()
-
-    def exchange(src, dst, k):
-        for d in range(1, NB):
-            peer = lax.rem(me + d, NB)
-            push(src.at[peer], dst.at[me], peer, k, "beam")
-
-    def gather(buf, k, n, my, axis):
-        for d in range(1, n):
-            push(buf.at[my], buf.at[my], lax.rem(my + d, n), k, axis)
-
-    def all_of(buf, k, n, axis):
-        part = buf.at[pl.ds(0, n - 1)]
+    H1, QA, ZB, PR, OO, LS, ZZ, HC = range(8)
+
+    def remote(src, dst, k, device):
         return pltpu.make_async_remote_copy(
-            src_ref=part, dst_ref=part, send_sem=ssem.at[k], recv_sem=rsem.at[k], device_id={axis: 0},
+            src_ref=src, dst_ref=dst, send_sem=ssem.at[k], recv_sem=rsem.at[k], device_id=device,
             device_id_type=MESH,
         )
 
-    def landed(buf, k, n=NB, axis="beam"):
-        all_of(buf, k, n, axis).wait_recv()
-
-    def sent(buf, k, n=NB, axis="beam"):
-        all_of(buf, k, n, axis).wait_send()
+    beam_peers = [((me + d) & (NB - 1), mt) for d in range(1, NB)]
+    tensor_peers = [(me, (mt + d) & (nt - 1)) for d in range(1, nt)]
+
+    def exchange(src, dst, k):
+        for peer in beam_peers:
+            remote(src.at[peer[0]], dst.at[me], k, peer).start()
+
+    def gather(buf, k, at, peers):
+        for peer in peers:
+            remote(buf.at[at], buf.at[at], k, peer).start()
+
+    def all_of(buf, k):
+        part = buf.at[pl.ds(0, buf.shape[0] - 1)]
+        return remote(part, part, k, (me, mt))
+
+    def landed(buf, k):
+        all_of(buf, k).wait_recv()
+
+    def sent(buf, k):
+        all_of(buf, k).wait_send()
 
     pairs = [
-        (par_h, par_ref), (cs_h, cs_ref), (cw_h, cw_ref), (q_h, q_ref), (s_h, s_v), (rates_h, rates_ref),
-        (x_h, x_ref), (cb_h, cb_ref), (po_h, po_ref), (ctx_h, ctx_ref), (xw_h, xw_v), (kv_h, kv_v),
+        (par_h, par_ref), (cs_h, cs_ref), (cw_h, cw_ref), (x_h, x_ref), (q_h, q_ref), (s_h, s_v),
+        (rates_h, rates_ref), (cb_h, cb_ref), (po_h, po_ref), (ctx_h, ctx_ref), (xw_h, xw_v), (kv_h, kv_v),
         (suf_h, suf_ref), (nkv_h, nkv_ref), (dtw_h, dtw_v), (dtb_h, dtb_ref), (gain_h, gain_ref),
         (skip_h, skip_ref), (gate_h, gate_ref),
     ]
     copies = [pltpu.make_async_copy(a, b, lsem.at[i]) for i, (a, b) in enumerate(pairs)]
-    (c_par, c_cs, c_cw, c_q, c_s, c_rates, c_x, c_cb, c_po, c_ctx, c_xw, c_kv, c_suf, c_nkv, c_dtw, c_dtb, c_gain,
+    (c_par, c_cs, c_cw, c_x, c_q, c_s, c_rates, c_cb, c_po, c_ctx, c_xw, c_kv, c_suf, c_nkv, c_dtw, c_dtb, c_gain,
      c_skip, c_gate) = copies
-    for c in copies:
+    for c in copies[0:5]:
         c.start()
     barrier = pltpu.get_barrier_semaphore()
-    for d in range(1, NB):
-        pl.semaphore_signal(barrier, inc=1, device_id={"beam": lax.rem(me + d, NB)}, device_id_type=MESH)
-    for d in range(1, nt):
-        pl.semaphore_signal(barrier, inc=1, device_id={"tensor": lax.rem(mt + d, nt)}, device_id_type=MESH)
+    greeted = beam_peers + tensor_peers
+    for peer in greeted:
+        pl.semaphore_signal(barrier, inc=1, device_id=peer, device_id_type=MESH)
+    for c in copies[5:]:
+        c.start()
 
     c_par.wait()
     par_t = par_ref[...].astype(f32).astype(bf16)
@@ -181,12 +181,15 @@
     win = [cs_ref[k].astype(f32) for k in range(3)]
     a0 = win[0] * cw_row[0] + win[1] * cw_row[1] + win[2] * cw_row[2]
     a1 = win[1] * cw_row[0] + win[2] * cw_row[1]
-    both = jnp.concatenate([to_rows(a0), to_rows(a1)], axis=1).astype(bf16)
-    packed = dot(pack_matrix(key0), both).astype(bf16)
-    h1s[...] = packed[:, 128:256].reshape(NB, 16, 128)
-    has[...] = packed[:, 0:128].reshape(NB, 16, 128)
+    h1s[:, 0:64, :] = jnp.broadcast_to(to_rows(a1).astype(bf16)[None], (NB, 64, 128))
+    h1s[:, 64:80, :] = dot(pack_matrix(key0), to_rows(a0).astype(bf16)).astype(bf16).reshape(NB, 16, 128)
+    key1 = slot_key(p1, me)
+    pb1 = pack_matrix(key1)
+    c_x.wait()
+    x0 = x_ref[0].astype(f32)
+    x1 = x_ref[1].astype(f32)
+    h1s[:, 80:96, :] = dot(pb1, to_rows(x0).astype(bf16)).astype(bf16).reshape(NB, 16, 128)
     h1r[pl.ds(me, 1)] = h1s[pl.ds(me, 1)]
-    har[pl.ds(me, 1)] = has[pl.ds(me, 1)]
 
     c_q.wait()
     qrows = jnp.concatenate(
@@ -196,37 +199,23 @@
     swap = one(((ri >> 3) == (ci & 7)) & ((ri & 7) == (ci >> 3)))
     qa[pl.ds(me, 1)] = dot(swap, qrows).astype(bf16)[None]
 
-    pl.semaphore_wait(barrier, NB - 1 + nt - 1)
+    pl.semaphore_wait(barrier, len(greeted))
 
     exchange(h1s, h1r, H1)
-    exchange(has, har, HA)
-
-    key1 = slot_key(p1, me)
-    pb1 = pack_matrix(key1)
+    gather(qa, QA, me, beam_peers)
+
     ub0 = unpack_matrix(p0, me)
     ub1 = unpack_matrix(p1, me)
     g = jnp.zeros((NB, REQ), i32)
     for p in range(NB):
         g = g + jnp.where(p1 == p, p0[p : p + 1, :], 0)
-    c_x.wait()
+    _, g_own = own_column(g, me)
+    g64 = jnp.concatenate([g_own] * LT, axis=0)
+    ai, aj = iota((64, NB * 64), 0), iota((64, NB * 64), 1)
+    ug = one((g64 == (aj >> 6).astype(f32)) & (ai == (aj & 63)))
     c_cb.wait()
-    x0 = x_ref[0].astype(f32)
-    x1 = x_ref[1].astype(f32)
     cb8 = cb_ref[...].astype(f32)
     cb = jnp.concatenate([cb8[i : i + 1] for i in range(LT)], axis=1)
-
-    landed(h1r, H1)
-    w1 = from_rows(dot(ub0, h1r[...].reshape(NB * 16, 128))) + cw_row[2] * x0
-    h2s[...] = dot(pb1, to_rows(w1).astype(bf16)).astype(bf16).reshape(NB, 16, 128)
-    h2r[pl.ds(me, 1)] = h2s[pl.ds(me, 1)]
-    exchange(h2s, h2r, H2)
-    gather(qa, QA, NB, me, "beam")
-
-    landed(har, HA)
-    c0 = from_rows(dot(ub0, har[...].reshape(NB * 16, 128))) + cw_row[3] * x0 + cb
-    conv0 = silu(c0)
-    hcs[...] = dot(pb1, to_rows(conv0).astype(bf16)).astype(bf16).reshape(NB, 16, 128)
-    hcr[pl.ds(me, 1)] = hcs[pl.ds(me, 1)]
 
     c_po.wait()
     c_ctx.wait()
@@ -284,12 +273,17 @@
     cp_tab.wait()
 
     c_xw.wait()
-    landed(h2r, H2)
-    conv1 = silu(from_rows(dot(ub1, h2r[...].reshape(NB * 16, 128))) + cw_row[3] * x1 + cb)
+    landed(h1r, H1)
+    conv0 = silu(from_rows(dot(ub0, h1r[:, 64:80, :].reshape(NB * 16, 128))) + cw_row[3] * x0 + cb)
+    older = from_rows(dot(ug, h1r[:, 0:64, :].reshape(NB * 64, 128)))
+    newer = from_rows(dot(ub1, h1r[:, 80:96, :].reshape(NB * 16, 128)))
+    conv1 = silu(older + cw_row[2] * newer + cw_row[3] * x1 + cb)
     part = dot_nt(jnp.concatenate([conv0, conv1], axis=0).astype(bf16), xw_v[...])
     zb[pl.ds(mt, 1)] = jnp.zeros((1, 16, PROJ_PAD), bf16)
     zb[pl.ds(mt, 1), :, 0:PROJ] = part.astype(bf16)[None]
-    gather(zb, ZB, nt, mt, "tensor")
+    gather(zb, ZB, mt, tensor_peers)
+    hcs[...] = dot(pb1, to_rows(conv0).astype(bf16)).astype(bf16).reshape(NB, 16, 128)
+    hcr[pl.ds(me, 1)] = hcs[pl.ds(me, 1)]
     exchange(hcs, hcr, HC)
 
 
@@ -352,12 +346,12 @@
     steps = NBLK // UNROLL
     lax.fori_loop(0, 2, blocks, 0)
 
-    landed(zb, ZB, nt, "tensor")
+    landed(zb, ZB)
     proj = jnp.zeros((16, PROJ_PAD), f32)
     for t in range(nt):
         proj = proj + zb[t].astype(f32)
     prb[pl.ds(me, 1)] = proj.astype(bf16)[None]
-    gather(prb, PR, NB, me, "beam")
+    gather(prb, PR, me, beam_peers)
 
     lax.fori_loop(2, steps, blocks, 0)
     c_suf.wait()
@@ -388,7 +382,7 @@
     os_[...] = osf[...].astype(bf16)
     or_[pl.ds(me, 1)] = os_[pl.ds(me, 1)]
     exchange(os_, or_, OO)
-    gather(lse, LS, NB, me, "beam")
+    gather(lse, LS, me, beam_peers)
 
     for c in (c_dtw, c_dtb, c_gain, c_skip, c_gate):
         c.wait()
@@ -455,7 +449,7 @@
     zzs[:, 64:80, :] = dot(relay, z0).astype(bf16).reshape(NB, 16, 128)
 
     def children(i, c):
-        two = [lax.rem(me + 1 + 2 * i, NB), lax.rem(me + 2 + 2 * i, NB)]
+        two = [(me + 1 + 2 * i) & (NB - 1), (me + 2 + 2 * i) & (NB - 1)]
         outs = [c1[b] for b in two]
         deltas = [d1[b] for b in two]
         accs = [jnp.zeros((REQ, CH), f32) for _ in two]
@@ -465,11 +459,11 @@
                 accs[k] = accs[k] + outs[k][:, DS + n : DS + n + 1] * (jnp.exp2(deltas[k] * rn) * sn)
         for k in range(2):
             zzs[two[k], 0:64, :] = to_rows(accs[k]).astype(bf16)
-        push(zzs.at[two[0]], zzr.at[me], two[0], ZZ, "beam")
+        remote(zzs.at[two[0]], zzr.at[me], ZZ, (two[0], mt)).start()
 
         @pl.when(i < NB // 2 - 1)
         def _():
-            push(zzs.at[two[1]], zzr.at[me], two[1], ZZ, "beam")
+            remote(zzs.at[two[1]], zzr.at[me], ZZ, (two[1], mt)).start()
 
         return c
 
@@ -529,11 +523,9 @@
     out_m.start()
 
     sent(h1s, H1)
-    sent(has, HA)
-    sent(h2s, H2)
     sent(hcs, HC)
     sent(qa, QA)
-    sent(zb, ZB, nt, "tensor")
+    sent(zb, ZB)
     sent(prb, PR)
     sent(os_, OO)
     sent(lse, LS)
@@ -618,12 +610,8 @@
         + [
             V(outs[0].shape, bf16),
             V(outs[1].shape, bf16),
-            V((NB, 16, 128), bf16),
-            V((NB, 16, 128), bf16),
-            V((NB, 16, 128), bf16),
-            V((NB, 16, 128), bf16),
-            V((NB, 16, 128), bf16),
-            V((NB, 16, 128), bf16),
+            V((NB, 96, 128), bf16),
+            V((NB, 96, 128), bf16),
             V((NB, 16, 128), bf16),
             V((NB, 16, 128), bf16),
             V((NB, 64, HD), bf16),
@@ -650,8 +638,8 @@
             V((128, REQ * 128), f32),
             dma((len(operands),)),
             dma,
-            dma((10,)),
-            dma((10,)),
+            dma((8,)),
+            dma((8,)),
         ],
         compiler_params=pltpu.CompilerParams(
             collective_id=0, has_side_effects=True, vmem_limit_bytes=63 * 2**20

time: 43.1 us -> 42.2 us (0.979)
  Pallas kernels: 41.7 us -> 40.9 us
    pallas_call x1, Pallas kernels: 40.4 us -> 39.5 us  [local(): pl.pallas_call(kernel, out_shape=outs, in_specs=[hb] * len(operands), out...]
where the time goes in v5:
time: 42.2 us; the launch traced here: 41.5 us
  Pallas kernels  40.9 us (97%)
  between operations  0.65 us (2%)
    pallas_call x1, Pallas kernels, local(): pl.pallas_call(kernel, out_shape=outs, in_specs=[hb] * len(operands), out...  39.5 us
    pallas_call x1, Pallas kernels, local(): pl.pallas_call(publish, out_shape=outs, in_specs=[hb, hb], out_specs=(hb,...  1.39 us

profile of v5, /device:TPU:2, one launch (start us, length us, event | category | flops | bytes accessed | tf_op | source)
XLA Modules:
  0.0 41.5 jit_solution(4088843901467872962)
XLA Ops:
  0.6 39.5 %decode.1 = (bf16[2,1,8,1024]{3,2,1,0:T(8,128)(2,1)}, bf16[2,1,8,512]{3,2,1,0:T(8,128)(2,1)}) custom-call(s32[16,16]{1,0:T(8,128)} %bitcast.26, s32[32,128]{1,0:T(8,128)} %bitcast.24, s32[8]{0:T(128)} %ctx_h.1, bf16[3,8,1024]{2,1,0:T(8,128)(2,1)} %bitcast.21, bf16[4,1024]{1,0:T(4,128)(2,1)} %cw_h.1, bf16[8,128]{1,0:T(8,128)(2,1)} %bitcast.30, ...), custom_call_target="tpu_custom_call" | custom-call | tf_op jit(solution)/shard_map/decode/pallas_call | solution.py:604
  40.1 1.4 %publish.1 = (bf16[2,1,8,1024]{3,2,1,0:T(8,128)(2,1)}, bf16[2,1,8,512]{3,2,1,0:T(8,128)(2,1)}) custom-call(bf16[2,1,8,1024]{3,2,1,0:T(8,128)(2,1)} %get-tuple-element.4.m_ref, bf16[2,1,8,512]{3,2,1,0:T(8,128)(2,1)} %get-tuple-element.5.a_ref), custom_call_target="tpu_custom_call" | custom-call | tf_op jit(solution)/shard_map/publish/pallas_call | solution.py:649

commit v6 on v5

--- a/solution.py
+++ b/solution.py
@@ -272,21 +272,6 @@
     mrun[0] = jnp.full((128, HD), NEG, f32)
     cp_tab.wait()
 
-    c_xw.wait()
-    landed(h1r, H1)
-    conv0 = silu(from_rows(dot(ub0, h1r[:, 64:80, :].reshape(NB * 16, 128))) + cw_row[3] * x0 + cb)
-    older = from_rows(dot(ug, h1r[:, 0:64, :].reshape(NB * 64, 128)))
-    newer = from_rows(dot(ub1, h1r[:, 80:96, :].reshape(NB * 16, 128)))
-    conv1 = silu(older + cw_row[2] * newer + cw_row[3] * x1 + cb)
-    part = dot_nt(jnp.concatenate([conv0, conv1], axis=0).astype(bf16), xw_v[...])
-    zb[pl.ds(mt, 1)] = jnp.zeros((1, 16, PROJ_PAD), bf16)
-    zb[pl.ds(mt, 1), :, 0:PROJ] = part.astype(bf16)[None]
-    gather(zb, ZB, mt, tensor_peers)
-    hcs[...] = dot(pb1, to_rows(conv0).astype(bf16)).astype(bf16).reshape(NB, 16, 128)
-    hcr[pl.ds(me, 1)] = hcs[pl.ds(me, 1)]
-    exchange(hcs, hcr, HC)
-
-
     wide = one((iota((REQ, REQ * 128), 1) >> 7) == iota((REQ, REQ * 128), 0))
     x_s0 = dot(one(p0 == me), wide)
     x_sg = dot(one(g == me), wide)
@@ -315,6 +300,32 @@
         sj = s_v[:, sl].astype(bf16)
         s0[:, :, sl] = dot(sel0, sj).reshape(DS, NB * 2, 256)
         s1[:, :, sl] = dot(perm1, sj).reshape(DS, REQ, 256)
+    held_here = column128(onef(g == me))
+    g1 = one((column128(p1) == (pj >> 3).astype(f32)) & ((pi & 7) == (pj & 7)))
+    r32 = one((iota((32, NB), 0) >> 1) == iota((32, NB), 1))
+    c32 = one((iota((REQ, 128), 1) & 7) == iota((REQ, 128), 0))
+    key32 = dot(dot(r32, key0.astype(bf16)).astype(bf16), c32)
+    si, sj_ = iota((32, 128), 0), iota((32, 128), 1)
+    psl = one((key32 == (si & 1).astype(f32)) & ((si >> 1) == (sj_ >> 3)))
+    ui, uj = iota((256, 256), 0), iota((256, 256), 1)
+    relay = one(((ui >> 4) == ((uj >> 1) & 15)) & (((ui >> 1) & 7) == (uj >> 5)) & ((ui & 1) == (uj & 1)))
+    _, own1 = own_column(p1, me)
+    gi, gj = iota((REQ, 128), 0), iota((REQ, 128), 1)
+    og = one((own1 == (gj >> 3).astype(f32)) & (gi == (gj & 7)))
+
+    c_xw.wait()
+    landed(h1r, H1)
+    conv0 = silu(from_rows(dot(ub0, h1r[:, 64:80, :].reshape(NB * 16, 128))) + cw_row[3] * x0 + cb)
+    older = from_rows(dot(ug, h1r[:, 0:64, :].reshape(NB * 64, 128)))
+    newer = from_rows(dot(ub1, h1r[:, 80:96, :].reshape(NB * 16, 128)))
+    conv1 = silu(older + cw_row[2] * newer + cw_row[3] * x1 + cb)
+    part = dot_nt(jnp.concatenate([conv0, conv1], axis=0).astype(bf16), xw_v[...])
+    zb[pl.ds(mt, 1)] = jnp.zeros((1, 16, PROJ_PAD), bf16)
+    zb[pl.ds(mt, 1), :, 0:PROJ] = part.astype(bf16)[None]
+    gather(zb, ZB, mt, tensor_peers)
+    hcs[...] = dot(pb1, to_rows(conv0).astype(bf16)).astype(bf16).reshape(NB, 16, 128)
+    hcr[pl.ds(me, 1)] = hcs[pl.ds(me, 1)]
+    exchange(hcs, hcr, HC)
 
 
     landed(qa, QA)
@@ -393,31 +404,6 @@
         return (rank_rows * lax.rsqrt(mean + 1e-6) * gain).astype(bf16)
 
     dtb = dtb_ref[...]
-    own = proj.astype(bf16).astype(f32)
-    d_own = softplus(dot(normed(own[:, 0:DT_RANK]), dtw_v[...]) + dtb)
-    d_own0, d_own1 = d_own[0:REQ], d_own[REQ : 2 * REQ]
-    own_in = own[:, DT_RANK : DT_RANK + DS]
-    own_out = own[:, DT_RANK + DS : DT_RANK + 2 * DS]
-    cb_own = jnp.sum(own_in * own_out, axis=1, keepdims=True)
-    skip = skip_ref[...]
-    base0 = d_own0 * conv0 * cb_own[0:REQ] + skip * conv0
-    base1 = d_own1 * conv1 * cb_own[REQ : 2 * REQ] + skip * conv1
-    gate0 = silu(gate_ref[0].astype(f32))
-    gate1 = silu(gate_ref[1].astype(f32))
-
-    held_here = column128(onef(g == me))
-    g1 = one((column128(p1) == (pj >> 3).astype(f32)) & ((pi & 7) == (pj & 7)))
-    r32 = one((iota((32, NB), 0) >> 1) == iota((32, NB), 1))
-    c32 = one((iota((REQ, 128), 1) & 7) == iota((REQ, 128), 0))
-    key32 = dot(dot(r32, key0.astype(bf16)).astype(bf16), c32)
-    si, sj_ = iota((32, 128), 0), iota((32, 128), 1)
-    psl = one((key32 == (si & 1).astype(f32)) & ((si >> 1) == (sj_ >> 3)))
-    ui, uj = iota((256, 256), 0), iota((256, 256), 1)
-    relay = one(((ui >> 4) == ((uj >> 1) & 15)) & (((ui >> 1) & 7) == (uj >> 5)) & ((ui & 1) == (uj & 1)))
-    _, own1 = own_column(p1, me)
-    gi, gj = iota((REQ, 128), 0), iota((REQ, 128), 1)
-    og = one((own1 == (gj >> 3).astype(f32)) & (gi == (gj & 7)))
-
     landed(prb, PR)
     prf = prb[...].astype(f32)
     pr0 = prf[:, 0:REQ, :].reshape(128, PROJ_PAD)
@@ -469,6 +455,18 @@
 
     lax.fori_loop(0, NB // 2, children, 0)
     zzr[pl.ds(me, 1)] = zzs[pl.ds(me, 1)]
+
+    own = proj.astype(bf16).astype(f32)
+    d_own = softplus(dot(normed(own[:, 0:DT_RANK]), dtw_v[...]) + dtb)
+    d_own0, d_own1 = d_own[0:REQ], d_own[REQ : 2 * REQ]
+    own_in = own[:, DT_RANK : DT_RANK + DS]
+    own_out = own[:, DT_RANK + DS : DT_RANK + 2 * DS]
+    cb_own = jnp.sum(own_in * own_out, axis=1, keepdims=True)
+    skip = skip_ref[...]
+    base0 = d_own0 * conv0 * cb_own[0:REQ] + skip * conv0
+    base1 = d_own1 * conv1 * cb_own[REQ : 2 * REQ] + skip * conv1
+    gate0 = silu(gate_ref[0].astype(f32))
+    gate1 = silu(gate_ref[1].astype(f32))
 
     landed(hcr, HC)
     conv0p = from_rows(dot(ub1, hcr[...].reshape(NB * 16, 128)))

time: 42.2 us -> 42.2 us (level)
  no operation moved by 1% of the time
where the time goes in v6:
time: 42.2 us; the launch traced here: 41.5 us
  Pallas kernels  40.9 us (97%)
  between operations  0.65 us (2%)
    pallas_call x1, Pallas kernels, local(): pl.pallas_call(kernel, out_shape=outs, in_specs=[hb] * len(operands), out...  39.5 us
    pallas_call x1, Pallas kernels, local(): pl.pallas_call(publish, out_shape=outs, in_specs=[hb, hb], out_specs=(hb,...  1.39 us

profile of v6, /device:TPU:2, one launch (start us, length us, event | category | flops | bytes accessed | tf_op | source)
XLA Modules:
  0.0 41.5 jit_solution(10990967850895784012)
XLA Ops:
  0.6 39.5 %decode.1 = (bf16[2,1,8,1024]{3,2,1,0:T(8,128)(2,1)}, bf16[2,1,8,512]{3,2,1,0:T(8,128)(2,1)}) custom-call(s32[16,16]{1,0:T(8,128)} %bitcast.26, s32[32,128]{1,0:T(8,128)} %bitcast.24, s32[8]{0:T(128)} %ctx_h.1, bf16[3,8,1024]{2,1,0:T(8,128)(2,1)} %bitcast.21, bf16[4,1024]{1,0:T(4,128)(2,1)} %cw_h.1, bf16[8,128]{1,0:T(8,128)(2,1)} %bitcast.30, ...), custom_call_target="tpu_custom_call" | custom-call | tf_op jit(solution)/shard_map/decode/pallas_call | solution.py:602
  40.1 1.4 %publish.1 = (bf16[2,1,8,1024]{3,2,1,0:T(8,128)(2,1)}, bf16[2,1,8,512]{3,2,1,0:T(8,128)(2,1)}) custom-call(bf16[2,1,8,1024]{3,2,1,0:T(8,128)(2,1)} %get-tuple-element.4.m_ref, bf16[2,1,8,512]{3,2,1,0:T(8,128)(2,1)} %get-tuple-element.5.a_ref), custom_call_target="tpu_custom_call" | custom-call | tf_op jit(solution)/shard_map/publish/pallas_call | solution.py:647

commit v7 on v6

--- a/solution.py
+++ b/solution.py
@@ -19,6 +19,10 @@
 BLK = 16
 NBLK = PAGES // BLK + REQ
 UNROLL = 8
+BEAM_ORDER = (
+    (2, 2), (2, 1), (1, 2), (2, -1), (-1, 2), (2, 0), (0, 2), (1, 1), (-1, -1), (1, -1), (-1, 1), (0, 1), (1, 0),
+    (0, -1), (-1, 0),
+)
 POOL = 4096
 PROJ = DT_RANK + 2 * DS
 PROJ_PAD = 384
@@ -129,8 +133,18 @@
             device_id_type=MESH,
         )
 
-    beam_peers = [((me + d) & (NB - 1), mt) for d in range(1, NB)]
-    tensor_peers = [(me, (mt + d) & (nt - 1)) for d in range(1, nt)]
+    core, mz, nz = mt & 1, mt >> 1, nt // 2
+    mx, my = me >> 2, me & 3
+
+    def beam_at(dx, dy):
+        return ((mx + dx + core * (-dy - dx)) & 3) * 4 + ((my + dy + core * (-dx - dy)) & 3)
+
+    def tensor_at(dz, other):
+        return ((mz + dz * (1 - 2 * core)) & (nz - 1)) * 2 + ((core + other) & 1)
+
+    beam_peers = [(beam_at(dx, dy), mt) for dx, dy in BEAM_ORDER]
+    z_order = [k for far in range(nz // 2, 0, -1) for k in sorted({far % nz, -far % nz})]
+    tensor_peers = [(me, tensor_at(dz, other)) for dz in z_order for other in (0, 1)] + [(me, tensor_at(0, 1))]
 
     def exchange(src, dst, k):
         for peer in beam_peers:
@@ -435,7 +449,8 @@
     zzs[:, 64:80, :] = dot(relay, z0).astype(bf16).reshape(NB, 16, 128)
 
     def children(i, c):
-        two = [(me + 1 + 2 * i) & (NB - 1), (me + 2 + 2 * i) & (NB - 1)]
+        two = [(turn >> 2, turn & 3) for turn in (NB - 1 - 2 * i, NB - 2 - 2 * i)]
+        two = [beam_at(dx, dy) for dx, dy in two]
         outs = [c1[b] for b in two]
         deltas = [d1[b] for b in two]
         accs = [jnp.zeros((REQ, CH), f32) for _ in two]

time: 42.2 us -> 40 us (0.948); the launches traced: 41.5 us -> 39.8 us
  Pallas kernels: 40.9 us -> 39.2 us
    pallas_call x1, Pallas kernels: 39.5 us -> 37.8 us  [local(): pl.pallas_call(kernel, out_shape=outs, in_specs=[hb] * len(operands), out...]
where the time goes in v7:
time: 40 us; the launch traced here: 39.8 us
  Pallas kernels  39.2 us (98%)
  between operations  0.65 us (2%)
    pallas_call x1, Pallas kernels, local(): pl.pallas_call(kernel, out_shape=outs, in_specs=[hb] * len(operands), out...  37.8 us
    pallas_call x1, Pallas kernels, local(): pl.pallas_call(publish, out_shape=outs, in_specs=[hb, hb], out_specs=(hb,...  1.39 us

profile of v7, /device:TPU:2, one launch (start us, length us, event | category | flops | bytes accessed | tf_op | source)
XLA Modules:
  0.0 39.8 jit_solution(9505776525355446826)
XLA Ops:
  0.6 37.8 %decode.1 = (bf16[2,1,8,1024]{3,2,1,0:T(8,128)(2,1)}, bf16[2,1,8,512]{3,2,1,0:T(8,128)(2,1)}) custom-call(s32[16,16]{1,0:T(8,128)} %bitcast.26, s32[32,128]{1,0:T(8,128)} %bitcast.24, s32[8]{0:T(128)} %ctx_h.1, bf16[3,8,1024]{2,1,0:T(8,128)(2,1)} %bitcast.21, bf16[4,1024]{1,0:T(4,128)(2,1)} %cw_h.1, bf16[8,128]{1,0:T(8,128)(2,1)} %bitcast.30, ...), custom_call_target="tpu_custom_call" | custom-call | tf_op jit(solution)/shard_map/decode/pallas_call | solution.py:617
  38.5 1.4 %publish.1 = (bf16[2,1,8,1024]{3,2,1,0:T(8,128)(2,1)}, bf16[2,1,8,512]{3,2,1,0:T(8,128)(2,1)}) custom-call(bf16[2,1,8,1024]{3,2,1,0:T(8,128)(2,1)} %get-tuple-element.4.m_ref, bf16[2,1,8,512]{3,2,1,0:T(8,128)(2,1)} %get-tuple-element.5.a_ref), custom_call_target="tpu_custom_call" | custom-call | tf_op jit(solution)/shard_map/publish/pallas_call | solution.py:662

commit v8 on v7

--- a/solution.py
+++ b/solution.py
@@ -449,7 +449,7 @@
     zzs[:, 64:80, :] = dot(relay, z0).astype(bf16).reshape(NB, 16, 128)
 
     def children(i, c):
-        two = [(turn >> 2, turn & 3) for turn in (NB - 1 - 2 * i, NB - 2 - 2 * i)]
+        two = [(turn & 3, ((turn >> 2) + turn) & 3) for turn in (NB - 1 - 2 * i, NB - 2 - 2 * i)]
         two = [beam_at(dx, dy) for dx, dy in two]
         outs = [c1[b] for b in two]
         deltas = [d1[b] for b in two]

time: 40 us -> 40.3 us (level)
  no operation moved by 1% of the time
where the time goes in v8:
time: 40.3 us; the launch traced here: 40.2 us
  Pallas kernels  39.5 us (98%)
  between operations  0.65 us (2%)
    pallas_call x1, Pallas kernels, local(): pl.pallas_call(kernel, out_shape=outs, in_specs=[hb] * len(operands), out...  38.1 us
    pallas_call x1, Pallas kernels, local(): pl.pallas_call(publish, out_shape=outs, in_specs=[hb, hb], out_specs=(hb,...  1.39 us

profile of v8, /device:TPU:2, one launch (start us, length us, event | category | flops | bytes accessed | tf_op | source)
XLA Modules:
  0.0 40.2 jit_solution(17776147559055043674)
XLA Ops:
  0.6 38.1 %decode.1 = (bf16[2,1,8,1024]{3,2,1,0:T(8,128)(2,1)}, bf16[2,1,8,512]{3,2,1,0:T(8,128)(2,1)}) custom-call(s32[16,16]{1,0:T(8,128)} %bitcast.26, s32[32,128]{1,0:T(8,128)} %bitcast.24, s32[8]{0:T(128)} %ctx_h.1, bf16[3,8,1024]{2,1,0:T(8,128)(2,1)} %bitcast.21, bf16[4,1024]{1,0:T(4,128)(2,1)} %cw_h.1, bf16[8,128]{1,0:T(8,128)(2,1)} %bitcast.30, ...), custom_call_target="tpu_custom_call" | custom-call | tf_op jit(solution)/shard_map/decode/pallas_call | solution.py:617
  38.8 1.4 %publish.1 = (bf16[2,1,8,1024]{3,2,1,0:T(8,128)(2,1)}, bf16[2,1,8,512]{3,2,1,0:T(8,128)(2,1)}) custom-call(bf16[2,1,8,1024]{3,2,1,0:T(8,128)(2,1)} %get-tuple-element.4.m_ref, bf16[2,1,8,512]{3,2,1,0:T(8,128)(2,1)} %get-tuple-element.5.a_ref), custom_call_target="tpu_custom_call" | custom-call | tf_op jit(solution)/shard_map/publish/pallas_call | solution.py:662

commit v9 on v7

--- a/solution.py
+++ b/solution.py
@@ -216,7 +216,6 @@
     pl.semaphore_wait(barrier, len(greeted))
 
     exchange(h1s, h1r, H1)
-    gather(qa, QA, me, beam_peers)
 
     ub0 = unpack_matrix(p0, me)
     ub1 = unpack_matrix(p1, me)
@@ -285,6 +284,8 @@
     orun[0] = jnp.zeros((128, 2 * HD), f32)
     mrun[0] = jnp.full((128, HD), NEG, f32)
     cp_tab.wait()
+
+    gather(qa, QA, me, beam_peers)
 
     wide = one((iota((REQ, REQ * 128), 1) >> 7) == iota((REQ, REQ * 128), 0))
     x_s0 = dot(one(p0 == me), wide)

time: 40 us -> 39.8 us (level)
  no operation moved by 1% of the time
where the time goes in v9:
time: 39.8 us; the launch traced here: 39.7 us
  Pallas kernels  39 us (98%)
  between operations  0.65 us (2%)
    pallas_call x1, Pallas kernels, local(): pl.pallas_call(kernel, out_shape=outs, in_specs=[hb] * len(operands), out...  37.6 us
    pallas_call x1, Pallas kernels, local(): pl.pallas_call(publish, out_shape=outs, in_specs=[hb, hb], out_specs=(hb,...  1.39 us

profile of v9, /device:TPU:2, one launch (start us, length us, event | category | flops | bytes accessed | tf_op | source)
XLA Modules:
  0.0 39.7 jit_solution(836250087955386812)
XLA Ops:
  0.6 37.6 %decode.1 = (bf16[2,1,8,1024]{3,2,1,0:T(8,128)(2,1)}, bf16[2,1,8,512]{3,2,1,0:T(8,128)(2,1)}) custom-call(s32[16,16]{1,0:T(8,128)} %bitcast.26, s32[32,128]{1,0:T(8,128)} %bitcast.24, s32[8]{0:T(128)} %ctx_h.1, bf16[3,8,1024]{2,1,0:T(8,128)(2,1)} %bitcast.21, bf16[4,1024]{1,0:T(4,128)(2,1)} %cw_h.1, bf16[8,128]{1,0:T(8,128)(2,1)} %bitcast.30, ...), custom_call_target="tpu_custom_call" | custom-call | tf_op jit(solution)/shard_map/decode/pallas_call | solution.py:618
  38.3 1.4 %publish.1 = (bf16[2,1,8,1024]{3,2,1,0:T(8,128)(2,1)}, bf16[2,1,8,512]{3,2,1,0:T(8,128)(2,1)}) custom-call(bf16[2,1,8,1024]{3,2,1,0:T(8,128)(2,1)} %get-tuple-element.4.m_ref, bf16[2,1,8,512]{3,2,1,0:T(8,128)(2,1)} %get-tuple-element.5.a_ref), custom_call_target="tpu_custom_call" | custom-call | tf_op jit(solution)/shard_map/publish/pallas_call | solution.py:663
